TPU v7x, 32 devices: a whole 2x2x4 slice. The times are simulated.
32 devices in a mesh: seq: 16 (over z, y, x), chan: 2 (over core).
Axes of the slice: x: 2, y: 2, z: 4, core: 2. Of those that a mesh axis runs over, the one named last changes fastest.
Arguments:
- query_in: bfloat16 [8192, 4096], P('seq', 'chan'), may hold values from -6 to 6
- key_in: bfloat16 [8192, 4096], P('seq', 'chan'), may hold values from -6 to 6
- value_in: bfloat16 [8192, 4096], P('seq', 'chan'), may hold values from -6 to 6
- decay_time: float32 [4096, 16], P('chan'), may hold values from 30 to 32768
- residue: float32 [4096, 16], P('chan'), may hold values from -27 to 27
- out_weight: bfloat16 [4096, 4096], P('chan'), may hold values from -0.09375 to 0.09375
- cotangent: bfloat16 [8192, 4096], P('seq', 'chan'), may hold values from -6 to 6
Outputs:
- mixed_out: bfloat16 [8192, 4096], P('seq', 'chan')
- query_grad: bfloat16 [8192, 4096], P('seq', 'chan')
- key_grad: bfloat16 [8192, 4096], P('seq', 'chan')
- value_grad: bfloat16 [8192, 4096], P('seq', 'chan')
- residue_grad: float32 [4096, 16], P('chan')
All inputs are finite; a program needn't handle non-finite values.
Results may differ from a plain program's by a relative error of at most 0.02.
Values may be sent and summed in bfloat16 or wider, within the bound.
A program may use at most 192 MiB of HBM per device.

v0:
```python
import math

import jax
import jax.numpy as jnp
from jax import lax
from jax.sharding import PartitionSpec as P

BLOCK = 128


HIGHEST_MODE = lax.Precision.HIGHEST
PREFIX_MODE = lax.Precision.HIGH


def combine(earlier, later):
    return (earlier[0] * later[0], later[0] * earlier[1] + later[1])


def group_width(channel_count, mode_count):
    return math.gcd(channel_count, max(1, 128 // mode_count))


def spread(rows, mode_count):
    channel_count = rows.shape[-1]
    width = group_width(channel_count, mode_count)
    lead = rows.shape[:-1]
    lanes_index = jnp.arange(width * mode_count) // mode_count
    spread_table = (jnp.arange(width)[:, None] == lanes_index[None, :]).astype(jnp.bfloat16)
    grouped = rows.reshape(lead + (channel_count // width, width))
    widened = jnp.einsum(
        "...gk,kl->...gl", grouped, spread_table, preferred_element_type=jnp.float32
    )
    return widened.reshape(lead + (channel_count * mode_count,))


def collapse(lanes, mode_count):
    lane_count = lanes.shape[-1]
    channel_count = lane_count // mode_count
    width = group_width(channel_count, mode_count)
    lead = lanes.shape[:-1]
    lanes_index = jnp.arange(width * mode_count) // mode_count
    sum_table = (lanes_index[:, None] == jnp.arange(width)[None, :]).astype(jnp.float32)
    grouped = lanes.reshape(lead + (channel_count // width, width * mode_count))
    summed = jnp.einsum("...gl,lk->...gk", grouped, sum_table, precision=HIGHEST_MODE)
    return summed.reshape(lead + (channel_count,))


def step_shape(block_count, lane_count, block_len):
    per_step = math.gcd(block_count, max(1, 2**21 // (lane_count * block_len)))
    return (per_step, block_count // per_step)


def local_pass(product_rows, weighted_rows, decay_rate, mode_gain, block_len):
    row_count, channel_count = product_rows.shape
    mode_count = decay_rate.shape[1]
    lane_count = channel_count * mode_count
    rate_flat = decay_rate.reshape(lane_count)
    gain_flat = mode_gain.reshape(lane_count)
    block_count = row_count // block_len
    per_step, step_count = step_shape(block_count, lane_count, block_len)
    offsets = jnp.arange(block_len, dtype=jnp.float32)[:, None]
    shrink = jnp.exp(-rate_flat[None, :] * offsets)
    growth = jnp.exp(rate_flat[None, :] * offsets)
    after_one = jnp.exp(-rate_flat[None, :] * (offsets + 1.0))
    lower_ones = (jnp.arange(block_len)[:, None] >= jnp.arange(block_len)[None, :]).astype(
        jnp.float32
    )
    upper_ones = lower_ones.T

    def one_step(correlation, inputs):
        product_part, weighted_part = inputs
        product_lanes = spread(product_part, mode_count)
        weighted_lanes = spread(weighted_part, mode_count)
        cumulated = jnp.einsum(
            "ij,gjm->gim", lower_ones, product_lanes * growth, precision=PREFIX_MODE
        )
        modal = cumulated * shrink
        conv_part = collapse(modal * gain_flat, mode_count)
        end_part = modal[:, block_len - 1]
        correlation = correlation + jnp.sum(modal * weighted_lanes, axis=(0, 1))
        after_part = jnp.sum(weighted_lanes * after_one, axis=1)
        back_cumulated = jnp.einsum(
            "ij,gjm->gim", upper_ones, weighted_lanes * shrink, precision=PREFIX_MODE
        )
        back_modal = back_cumulated * growth
        back_part = collapse(back_modal * gain_flat, mode_count)
        start_part = back_modal[:, 0]
        return (correlation, (conv_part, back_part, end_part, start_part, after_part))

    shaped_product = product_rows.reshape(step_count, per_step, block_len, channel_count)
    shaped_weighted = weighted_rows.reshape(step_count, per_step, block_len, channel_count)
    correlation, stacked = lax.scan(
        one_step, jnp.zeros((lane_count,), jnp.float32), (shaped_product, shaped_weighted)
    )
    conv_local = stacked[0].reshape(block_count, block_len, channel_count)
    back_local = stacked[1].reshape(block_count, block_len, channel_count)
    end_states = stacked[2].reshape(block_count, lane_count)
    start_states = stacked[3].reshape(block_count, lane_count)
    after_sums = stacked[4].reshape(block_count, lane_count)
    block_decay = jnp.broadcast_to(jnp.exp(-rate_flat * block_len), end_states.shape)
    forward_prefix = lax.associative_scan(combine, (block_decay, end_states), axis=0)[1]
    backward_suffix = lax.associative_scan(
        combine, (block_decay, start_states), reverse=True, axis=0
    )[1]
    return (correlation, conv_local, back_local, forward_prefix, backward_suffix, after_sums)


def finish(parts, decay_rate, mode_gain, block_len, carry_in, carry_back):
    correlation, conv_local, back_local, forward_prefix, backward_suffix, after_sums = parts
    block_count, _, channel_count = conv_local.shape
    mode_count = decay_rate.shape[1]
    lane_count = channel_count * mode_count
    rate_flat = decay_rate.reshape(lane_count)
    gain_flat = mode_gain.reshape(lane_count)
    block_pos = jnp.arange(block_count, dtype=jnp.float32)[:, None]
    empty_row = jnp.zeros((1, lane_count), jnp.float32)
    incoming = (
        jnp.concatenate([empty_row, forward_prefix[:-1]], axis=0)
        + jnp.exp(-rate_flat * block_len * block_pos) * carry_in
    )
    outgoing = (
        jnp.concatenate([backward_suffix[1:], empty_row], axis=0)
        + jnp.exp(-rate_flat * block_len * (block_count - 1.0 - block_pos)) * carry_back
    )
    offsets = jnp.arange(block_len, dtype=jnp.float32)[:, None]
    after_table = gain_flat * jnp.exp(-rate_flat * (offsets + 1.0))
    before_table = gain_flat * jnp.exp(-rate_flat * (block_len - offsets))
    per_step, step_count = step_shape(block_count, lane_count, block_len)

    def corrections(states):
        incoming_part, outgoing_part = states
        conv_add = collapse(after_table[None] * incoming_part[:, None, :], mode_count)
        back_add = collapse(before_table[None] * outgoing_part[:, None, :], mode_count)
        return (conv_add, back_add)

    conv_add, back_add = lax.map(
        corrections,
        (
            incoming.reshape(step_count, per_step, lane_count),
            outgoing.reshape(step_count, per_step, lane_count),
        ),
    )
    conv_total = conv_local + conv_add.reshape(block_count, block_len, channel_count)
    back_total = back_local + back_add.reshape(block_count, block_len, channel_count)
    correlation = (correlation + jnp.sum(incoming * after_sums, axis=0)).reshape(
        channel_count, mode_count
    )
    row_count = block_count * block_len
    return (
        conv_total.reshape(row_count, channel_count),
        back_total.reshape(row_count, channel_count),
        correlation,
    )


def per_device(query_in, key_in, value_in, decay_time, residue, out_weight, cotangent):
    decay_rate = 1.0 / decay_time
    norm_factor = jnp.sqrt(-jnp.expm1(-2.0 * decay_rate))
    mode_gain = norm_factor * residue
    seq_count = lax.axis_size("seq")
    row_count, channel_count = query_in.shape
    mode_count = decay_rate.shape[1]
    scale_factor = norm_factor / jnp.sqrt(jnp.float32(row_count * seq_count))
    grad_gated = lax.dot_general(
        lax.all_gather(cotangent, "chan", axis=1, tiled=True),
        out_weight,
        (((1,), (1,)), ((), ())),
        preferred_element_type=jnp.float32,
    )
    query_wide = query_in.astype(jnp.float32)
    product = (key_in.astype(jnp.float32) * value_in.astype(jnp.float32)).astype(jnp.bfloat16)
    weighted = (grad_gated * query_wide).astype(jnp.bfloat16)
    moved_product, moved_weighted = (
        lax.all_to_all(product, "seq", split_axis=1, concat_axis=0, tiled=True),
        lax.all_to_all(weighted, "seq", split_axis=1, concat_axis=0, tiled=True),
    )
    part_width = channel_count // seq_count
    first = lax.axis_index("seq") * part_width
    rate_part = lax.dynamic_slice_in_dim(decay_rate, first, part_width, 0)
    gain_part = lax.dynamic_slice_in_dim(mode_gain, first, part_width, 0)
    scale_part = lax.dynamic_slice_in_dim(scale_factor, first, part_width, 0)
    parts = local_pass(moved_product, moved_weighted, rate_part, gain_part, BLOCK)
    no_carry = jnp.zeros((part_width * mode_count,), jnp.float32)
    conv_full, back_full, correlation = finish(
        parts, rate_part, gain_part, BLOCK, no_carry, no_carry
    )
    convolved, grad_product = (
        lax.all_to_all(
            conv_full.astype(jnp.bfloat16), "seq", split_axis=0, concat_axis=1, tiled=True
        ).astype(conv_full.dtype),
        lax.all_to_all(
            back_full.astype(jnp.bfloat16), "seq", split_axis=0, concat_axis=1, tiled=True
        ).astype(back_full.dtype),
    )
    residue_grad = lax.all_gather(scale_part * correlation, "seq", axis=0, tiled=True)
    gated = (query_wide * convolved).astype(jnp.bfloat16)
    partial_out = jnp.dot(gated, out_weight, preferred_element_type=jnp.float32)
    mixed_out = lax.psum_scatter(
        partial_out.astype(jnp.bfloat16), "chan", scatter_dimension=1, tiled=True
    )
    query_grad = (grad_gated * convolved).astype(jnp.bfloat16)
    key_grad = (grad_product * value_in.astype(jnp.float32)).astype(jnp.bfloat16)
    value_grad = (grad_product * key_in.astype(jnp.float32)).astype(jnp.bfloat16)
    return (mixed_out, query_grad, key_grad, value_grad, residue_grad)


def solution(mesh):
    in_specs = (
        P("seq", "chan"),
        P("seq", "chan"),
        P("seq", "chan"),
        P("chan", None),
        P("chan", None),
        P("chan", None),
        P("seq", "chan"),
    )
    out_specs = (
        P("seq", "chan"),
        P("seq", "chan"),
        P("seq", "chan"),
        P("seq", "chan"),
        P("chan", None),
    )
    return jax.shard_map(
        per_device, mesh=mesh, in_specs=in_specs, out_specs=out_specs, check_vma=False
    )
```

profile of v0, /device:TPU:0, one launch (start us, length us, event | category | flops | bytes accessed | tf_op | source)
XLA Modules:
  0.0 1601.8 jit_solution(12213431713968694575)
XLA Ops:
  44.3 26.0 %all-to-all-done = bf16[512,16,128]{0,2,1:T(8,128)(2,1)S(1)} async-done(((bf16[512,16,128]{0,2,1:T(8,128)(2,1)}), bf16[512,16,128]{0,2,1:T(8,128)(2,1)S(1)}, u32[]{:S(2)}, u32[]{:S(2)}) %all-to-all-start) | async-done | bytes 2097184 | tf_op jit(solution)/shard_map/all_to_all | solution.py:174
  97.7 25.1 %all-to-all-done.1 = bf16[512,16,128]{2,0,1:T(8,128)(2,1)} async-done(((bf16[512,16,128]{2,0,1:T(8,128)(2,1)}), bf16[512,16,128]{2,0,1:T(8,128)(2,1)}, u32[]{:S(2)}, u32[]{:S(2)}) %all-to-all-start.1) | async-done | bytes 2097184 | tf_op jit(solution)/shard_map/all_to_all | solution.py:175
  127.9 1165.1 %while.43 = (s32[]{:T(128)}, f32[2048]{0:T(1024)S(1)}, f32[8,8,128,128]{3,2,1,0:T(8,128)}, f32[8,8,128,128]{3,2,1,0:T(8,128)}, f32[8,8,2048]{2,1,0:T(8,128)}, /*...) while((s32[]{:T(128)}, f32[2048]{0:T(1024)S(1)}, ...), condition=%wide.wide.region_3.4_spmd.clone.clone.clone, body=%wide.wide.region_0.3_spmd.clone.clone.clone.sunk | while | flops 3712801792 | bytes 220597472 | solution.py:92
  194.4 31.6 %fusion.140 = f32[8,128,16,8]{2,3,1,0:T(8,128)} fusion(s32[128]{0:T(128)S(1)} %and_select_fusion.6, f32[8,128,16,128]{3,2,1,0:T(8,128)S(1)} %bitcast.207), kind=kOutput, calls=%fused_computation.35.clone.clone.1 | convolution fusion | flops 201327616 | bytes 8913408 | tf_op jit(solution)/shard_map/while/body/eval_jaxpr/...gl,lk->...gk/dot_general | solution.py:44
  237.6 31.5 %fusion.141 = f32[8,128,16,8]{2,3,1,0:T(8,128)} fusion(s32[128]{0:T(128)S(1)} %and_select_fusion.6, f32[8,128,16,128]{3,2,1,0:T(8,128)S(1)} %bitcast.205), kind=kOutput, calls=%fused_computation.33.clone.clone.1 | convolution fusion | flops 201327616 | bytes 8913408 | tf_op jit(solution)/shard_map/while/body/eval_jaxpr/...gl,lk->...gk/dot_general | solution.py:44
  339.4 31.8 %fusion.140 = f32[8,128,16,8]{2,3,1,0:T(8,128)} fusion(s32[128]{0:T(128)S(1)} %and_select_fusion.6, f32[8,128,16,128]{3,2,1,0:T(8,128)S(1)} %bitcast.207), kind=kOutput, calls=%fused_computation.35.clone.clone.1 | convolution fusion | flops 201327616 | bytes 8913408 | tf_op jit(solution)/shard_map/while/body/eval_jaxpr/...gl,lk->...gk/dot_general | solution.py:44
  382.8 31.4 %fusion.141 = f32[8,128,16,8]{2,3,1,0:T(8,128)} fusion(s32[128]{0:T(128)S(1)} %and_select_fusion.6, f32[8,128,16,128]{3,2,1,0:T(8,128)S(1)} %bitcast.205), kind=kOutput, calls=%fused_computation.33.clone.clone.1 | convolution fusion | flops 201327616 | bytes 8913408 | tf_op jit(solution)/shard_map/while/body/eval_jaxpr/...gl,lk->...gk/dot_general | solution.py:44
  461.0 18.3 %broadcast_multiply_fusion.5 = (f32[8,128,2048]{2,1,0:T(8,128)}, f32[2048]{0:T(1024)S(1)}, f32[8,128,2048]{2,1,0:T(8,128)}, f32[8,128,2048]{2,1,0:T(8,128)}) fusion(f32[2048]{0:T(1024)S(1)} %get-tuple-element.953, f32[8,128,2048]{2,1,0:T(8,128)} %copy.255, f32[8,128,2048]{2,1,0:T(8,128)} %copy-done, f32[128,2048]{1,0:T(8,128)S(1)} %get-tuple-element.900, ...), kind=kOutput, calls=%fused_computation.46.clone.clone.1 | convolution fusion | flops 1623226368 | bytes 52445184 | tf_op jit(solution)/shard_map/while/body/eval_jaxpr/ij,gjm->gim/dot_general | solution.py:74
  484.7 31.6 %fusion.140 = f32[8,128,16,8]{2,3,1,0:T(8,128)} fusion(s32[128]{0:T(128)S(1)} %and_select_fusion.6, f32[8,128,16,128]{3,2,1,0:T(8,128)S(1)} %bitcast.207), kind=kOutput, calls=%fused_computation.35.clone.clone.1 | convolution fusion | flops 201327616 | bytes 8913408 | tf_op jit(solution)/shard_map/while/body/eval_jaxpr/...gl,lk->...gk/dot_general | solution.py:44
  527.9 31.5 %fusion.141 = f32[8,128,16,8]{2,3,1,0:T(8,128)} fusion(s32[128]{0:T(128)S(1)} %and_select_fusion.6, f32[8,128,16,128]{3,2,1,0:T(8,128)S(1)} %bitcast.205), kind=kOutput, calls=%fused_computation.33.clone.clone.1 | convolution fusion | flops 201327616 | bytes 8913408 | tf_op jit(solution)/shard_map/while/body/eval_jaxpr/...gl,lk->...gk/dot_general | solution.py:44
  629.7 31.8 %fusion.140 = f32[8,128,16,8]{2,3,1,0:T(8,128)} fusion(s32[128]{0:T(128)S(1)} %and_select_fusion.6, f32[8,128,16,128]{3,2,1,0:T(8,128)S(1)} %bitcast.207), kind=kOutput, calls=%fused_computation.35.clone.clone.1 | convolution fusion | flops 201327616 | bytes 8913408 | tf_op jit(solution)/shard_map/while/body/eval_jaxpr/...gl,lk->...gk/dot_general | solution.py:44
  673.1 31.4 %fusion.141 = f32[8,128,16,8]{2,3,1,0:T(8,128)} fusion(s32[128]{0:T(128)S(1)} %and_select_fusion.6, f32[8,128,16,128]{3,2,1,0:T(8,128)S(1)} %bitcast.205), kind=kOutput, calls=%fused_computation.33.clone.clone.1 | convolution fusion | flops 201327616 | bytes 8913408 | tf_op jit(solution)/shard_map/while/body/eval_jaxpr/...gl,lk->...gk/dot_general | solution.py:44
  751.2 18.3 %broadcast_multiply_fusion.5 = (f32[8,128,2048]{2,1,0:T(8,128)}, f32[2048]{0:T(1024)S(1)}, f32[8,128,2048]{2,1,0:T(8,128)}, f32[8,128,2048]{2,1,0:T(8,128)}) fusion(f32[2048]{0:T(1024)S(1)} %get-tuple-element.953, f32[8,128,2048]{2,1,0:T(8,128)} %copy.255, f32[8,128,2048]{2,1,0:T(8,128)} %copy-done, f32[128,2048]{1,0:T(8,128)S(1)} %get-tuple-element.900, ...), kind=kOutput, calls=%fused_computation.46.clone.clone.1 | convolution fusion | flops 1623226368 | bytes 52445184 | tf_op jit(solution)/shard_map/while/body/eval_jaxpr/ij,gjm->gim/dot_general | solution.py:74
  775.0 31.6 %fusion.140 = f32[8,128,16,8]{2,3,1,0:T(8,128)} fusion(s32[128]{0:T(128)S(1)} %and_select_fusion.6, f32[8,128,16,128]{3,2,1,0:T(8,128)S(1)} %bitcast.207), kind=kOutput, calls=%fused_computation.35.clone.clone.1 | convolution fusion | flops 201327616 | bytes 8913408 | tf_op jit(solution)/shard_map/while/body/eval_jaxpr/...gl,lk->...gk/dot_general | solution.py:44
  818.2 31.5 %fusion.141 = f32[8,128,16,8]{2,3,1,0:T(8,128)} fusion(s32[128]{0:T(128)S(1)} %and_select_fusion.6, f32[8,128,16,128]{3,2,1,0:T(8,128)S(1)} %bitcast.205), kind=kOutput, calls=%fused_computation.33.clone.clone.1 | convolution fusion | flops 201327616 | bytes 8913408 | tf_op jit(solution)/shard_map/while/body/eval_jaxpr/...gl,lk->...gk/dot_general | solution.py:44
  920.0 31.8 %fusion.140 = f32[8,128,16,8]{2,3,1,0:T(8,128)} fusion(s32[128]{0:T(128)S(1)} %and_select_fusion.6, f32[8,128,16,128]{3,2,1,0:T(8,128)S(1)} %bitcast.207), kind=kOutput, calls=%fused_computation.35.clone.clone.1 | convolution fusion | flops 201327616 | bytes 8913408 | tf_op jit(solution)/shard_map/while/body/eval_jaxpr/...gl,lk->...gk/dot_general | solution.py:44
  963.4 31.4 %fusion.141 = f32[8,128,16,8]{2,3,1,0:T(8,128)} fusion(s32[128]{0:T(128)S(1)} %and_select_fusion.6, f32[8,128,16,128]{3,2,1,0:T(8,128)S(1)} %bitcast.205), kind=kOutput, calls=%fused_computation.33.clone.clone.1 | convolution fusion | flops 201327616 | bytes 8913408 | tf_op jit(solution)/shard_map/while/body/eval_jaxpr/...gl,lk->...gk/dot_general | solution.py:44
  1065.3 31.6 %fusion.140 = f32[8,128,16,8]{2,3,1,0:T(8,128)} fusion(s32[128]{0:T(128)S(1)} %and_select_fusion.6, f32[8,128,16,128]{3,2,1,0:T(8,128)S(1)} %bitcast.207), kind=kOutput, calls=%fused_computation.35.clone.clone.1 | convolution fusion | flops 201327616 | bytes 8913408 | tf_op jit(solution)/shard_map/while/body/eval_jaxpr/...gl,lk->...gk/dot_general | solution.py:44
  1108.5 31.5 %fusion.141 = f32[8,128,16,8]{2,3,1,0:T(8,128)} fusion(s32[128]{0:T(128)S(1)} %and_select_fusion.6, f32[8,128,16,128]{3,2,1,0:T(8,128)S(1)} %bitcast.205), kind=kOutput, calls=%fused_computation.33.clone.clone.1 | convolution fusion | flops 201327616 | bytes 8913408 | tf_op jit(solution)/shard_map/while/body/eval_jaxpr/...gl,lk->...gk/dot_general | solution.py:44
  1210.3 31.8 %fusion.140 = f32[8,128,16,8]{2,3,1,0:T(8,128)} fusion(s32[128]{0:T(128)S(1)} %and_select_fusion.6, f32[8,128,16,128]{3,2,1,0:T(8,128)S(1)} %bitcast.207), kind=kOutput, calls=%fused_computation.35.clone.clone.1 | convolution fusion | flops 201327616 | bytes 8913408 | tf_op jit(solution)/shard_map/while/body/eval_jaxpr/...gl,lk->...gk/dot_general | solution.py:44
  1253.7 31.4 %fusion.141 = f32[8,128,16,8]{2,3,1,0:T(8,128)} fusion(s32[128]{0:T(128)S(1)} %and_select_fusion.6, f32[8,128,16,128]{3,2,1,0:T(8,128)S(1)} %bitcast.205), kind=kOutput, calls=%fused_computation.33.clone.clone.1 | convolution fusion | flops 201327616 | bytes 8913408 | tf_op jit(solution)/shard_map/while/body/eval_jaxpr/...gl,lk->...gk/dot_general | solution.py:44
  1310.5 102.0 %while.42 = (s32[]{:T(128)}, f32[8,8,128,128]{3,2,1,0:T(8,128)}, f32[8,8,128,128]{3,2,1,0:T(8,128)}, f32[8,8,2048]{2,1,0:T(8,128)}, f32[8,8,2048]{2,1,0:T(8,128)...) while((s32[]{:T(128)}, f32[8,8,128,128]{3,2,1,0:T(8,128)}, ...), condition=%wide.region_5.6_spmd.clone.clone, body=%wide.region_4.5_spmd.clone.clone.sunk | while | flops 407899136 | bytes 14305913 | solution.py:136
  1416.9 58.0 %all_to_all.52 = bf16[16,512,128]{2,1,0:T(8,128)(2,1)S(1)} all-to-all(bf16[16,512,128]{2,1,0:T(8,128)(2,1)S(1)} %bitcast.217), channel_id=1, replica_groups=mesh['seq'=16,'chan'=2] {'seq'}, dimensions={0} | all-to-all | bytes 4194304 | tf_op jit(solution)/shard_map/all_to_all | solution.py:188
  1500.6 67.6 %all_gather.7 = f32[2048,16]{0,1:T(8,128)S(1)} all-gather(f32[128,16]{0,1:T(8,128)S(1)} %multiply_multiply_fusion.1), channel_id=1, replica_groups=mesh['seq'=16,'chan'=2] {'seq'}, dimensions={0}, use_global_device_ids=true | all-gather | bytes 139264 | tf_op jit(solution)/shard_map/all_gather | solution.py:195
  (557 shorter events, 859.8 us)
Async XLA Ops:
  7.2 20.2 %all-gather.2.cloned.1.call-start = ((), (), s32[]{:S(2)}) async-start(), calls=%async_computation.5 | async-start | bytes 6291456 | tf_op jit(solution)/shard_map/all_gather | solution.py:165
  10.8 8.1 copy-start.1
  18.9 51.5 %all-to-all-start = ((bf16[512,16,128]{0,2,1:T(8,128)(2,1)}), bf16[512,16,128]{0,2,1:T(8,128)(2,1)S(1)}, u32[]{:S(2)}, u32[]{:S(2)}) async-start(bf16[512,16,128]{0,2,1:T(8,128)(2,1)} %bitcast.216), calls=%async_computation | async-start | bytes 4194304 | tf_op jit(solution)/shard_map/all_to_all | solution.py:174
  27.4 15.1 copy-start.6
  44.3 36.0 %copy-start.17 = (f32[2048,16]{0,1:T(8,128)S(1)}, f32[2048,16]{0,1:T(8,128)}, u32[]{:S(2)}) copy-start(f32[2048,16]{0,1:T(8,128)} %param.14) | copy-start | bytes 393220
  70.3 52.5 %all-to-all-start.1 = ((bf16[512,16,128]{2,0,1:T(8,128)(2,1)}), bf16[512,16,128]{2,0,1:T(8,128)(2,1)}, u32[]{:S(2)}, u32[]{:S(2)}) async-start(bf16[512,16,128]{2,0,1:T(8,128)(2,1)} %copy_bitcast_fusion.2), calls=%async_computation.1 | async-start | bytes 4194304 | tf_op jit(solution)/shard_map/all_to_all | solution.py:175
  80.2 1513.9 %reduce-scatter.2.cloned.1.call-start = ((), (), s32[]{:S(2)}) async-start(), calls=%async_computation.6 | async-start | bytes 6291456 | tf_op jit(solution)/shard_map/reduce_scatter | solution.py:198
  84.3 41.1 %copy-start.14 = (f32[2048]{0:T(1024)}, f32[2048]{0:T(1024)S(1)}, u32[]{:S(2)}) copy-start(f32[2048]{0:T(1024)S(1)} %get-tuple-element.676) | copy-start | bytes 24580
  127.9 1169.4 %copy-start.15 = (f32[2048]{0:T(1024)S(1)}, f32[2048]{0:T(1024)}, u32[]{:S(2)}) copy-start(f32[2048]{0:T(1024)} %copy-done.14) | copy-start | bytes 24580
  127.9 1169.7 %copy-start.18 = (f32[2048]{0:T(1024)S(1)}, f32[2048]{0:T(1024)}, u32[]{:S(2)}) copy-start(f32[2048]{0:T(1024)} %get-tuple-element.672) | copy-start | bytes 24580
  127.9 1169.8 %copy-start.20 = (f32[2048]{0:T(1024)S(1)}, f32[2048]{0:T(1024)}, u32[]{:S(2)}) copy-start(f32[2048]{0:T(1024)} %get-tuple-element.673) | copy-start | bytes 24580
  312.7 3.2 copy-start
  893.2 3.2 copy-start
  1293.1 4.8 copy-start.21
  1293.1 4.9 copy-start.23
  1293.1 4.9 copy-start.19
  1293.1 5.0 copy-start.9
  1293.1 6.1 copy-start.11
  1305.5 5.0 copy-start.13
  1305.5 5.0 copy-start.24
  1416.9 59.4 %copy-start.7 = (bf16[512,2048]{1,0:T(8,128)(2,1)S(1)}, bf16[512,2048]{1,0:T(8,128)(2,1)}, u32[]{:S(2)}) copy-start(bf16[512,2048]{1,0:T(8,128)(2,1)} %param.11) | copy-start | bytes 6291460
  1495.9 72.3 %all-to-all-start.3 = ((bf16[16,512,128]{2,1,0:T(8,128)(2,1)}), bf16[16,512,128]{2,1,0:T(8,128)(2,1)S(1)}, u32[]{:S(2)}, u32[]{:S(2)}) async-start(bf16[16,512,128]{2,1,0:T(8,128)(2,1)} %bitcast.215), calls=%async_computation.4 | async-start | bytes 4194304 | tf_op jit(solution)/shard_map/all_to_all | solution.py:191
  1570.7 5.6 copy-start.2
  1582.1 8.0 copy-start.5
  (15 other events, 32.7 us)
Sparse Core Ops, SparseCore 0:
  9.5 16.3 all-gather.1
  1490.3 10.2 reduce-scatter.1
where the time goes:
time: 1610 us; the launch traced here: 1600 us
  matrix products  890 us (55%)
  local copies, waits for them, and re-layouts  444 us (28%)
  blocking collectives  126 us (8%)
  waiting for transfers between devices  51.9 us (3%)
  other arithmetic  44.5 us (3%)
  starting transfers between devices  22.3 us (1%)
    dot_general x32, matrix products, collapse(): jnp.einsum('...gl,lk->...gk', grouped, sum_table, precision=HIGHEST_MODE)  572 us
    reshape x16, local copies, waits for them, and re-layouts, spread(): return widened.reshape(lead + (channel_count * mode_count,))  146 us
    dot_general x8, matrix products, one_step(): jnp.einsum('ij,gjm->gim', lower_ones, product_lanes * growth, precision=P...  145 us
    while x56, local copies, waits for them, and re-layouts  119 us
    dot_general x16, matrix products, spread(): jnp.einsum('...gk,kl->...gl', grouped, spread_table, preferred_element_ty...  82.5 us
    all_gather x1, blocking collectives, per_device(): lax.all_gather(scale_part * correlation, 'seq', axis=0, tiled=True)  67.6 us
    dot_general x8, matrix products, one_step(): jnp.einsum('ij,gjm->gim', upper_ones, weighted_lanes * shrink, precision=...  63.7 us
    all_to_all x1, blocking collectives, per_device(): lax.all_to_all(conv_full.astype(jnp.bfloat16), 'seq', split_axis=0, conca...  58 us
  transfers between devices with their start and end apart: 5, of which 2 were waited for; matrix products, arithmetic and copies ran while one was open for 5% of the time, Pallas kernels for 0%

commit v1 on v0

v1 whole, which is shorter than its diff:
```python
import functools

import jax
import jax.numpy as jnp
from jax import lax
from jax.experimental import pallas as pl
from jax.experimental.pallas import tpu as pltpu
from jax.sharding import PartitionSpec as P

LANES = 128
BLOCKS = 8
UNROLL = 8
F32 = jnp.float32
BF16 = jnp.bfloat16


def tree_sum(terms):
    while len(terms) > 1:
        pairs = [terms[i] + terms[i + 1] for i in range(0, len(terms) - 1, 2)]
        terms = pairs + terms[len(terms) - len(terms) % 2 :]
    return terms[0]


def row(ref, t, steps):
    return ref[pl.ds(t, BLOCKS, stride=steps), :]


def spread_rows(rate, first, count):
    return [
        jnp.broadcast_to(rate[n : n + 1, :], (BLOCKS, LANES)) for n in range(first, first + count)
    ]


def run_states(source, decays, steps, backward):
    def body(outer, states):
        for inner in range(UNROLL):
            t = outer * UNROLL + inner
            x = row(source, steps - 1 - t if backward else t, steps)
            states = [d * s + x for d, s in zip(decays, states)]
        return states

    zeros = [jnp.zeros((BLOCKS, LANES), F32) for _ in decays]
    return lax.fori_loop(0, steps // UNROLL, body, zeros)


def join_blocks(ends, rate, steps, backward):
    modes = rate.shape[0]
    step_decay = jnp.exp(-rate * float(steps))
    total = jnp.zeros((modes, LANES), F32)
    for b in reversed(range(BLOCKS)) if backward else range(BLOCKS):
        total = total * step_decay + ends[pl.ds(b, modes, stride=BLOCKS), :]
    return total


def block_carries(gathered, ends, rate, place, steps, carries, backward):
    modes = rate.shape[0]
    count = gathered.shape[0]
    step_decay = jnp.exp(-rate * float(steps))
    device_decay = jnp.exp(-rate * float(steps * BLOCKS))
    run = jnp.zeros((modes, LANES), F32)
    for e in reversed(range(count)) if backward else range(count):
        kept = place < e if backward else place > e
        run = jnp.where(kept, run * device_decay + gathered[e], run)
    for b in reversed(range(BLOCKS)) if backward else range(BLOCKS):
        carries[pl.ds(b, modes, stride=BLOCKS), :] = run
        run = run * step_decay + ends[pl.ds(b, modes, stride=BLOCKS), :]


def forward_ends_kernel(key_ref, value_ref, rate_ref, ends_ref, total_ref, source):
    steps = key_ref.shape[0] // BLOCKS
    rate = rate_ref[...]
    modes = rate.shape[0]
    source[...] = (key_ref[...].astype(F32) * value_ref[...].astype(F32)).astype(BF16).astype(F32)
    decays = spread_rows(jnp.exp(-rate), 0, modes)
    for n, state in enumerate(run_states(source, decays, steps, False)):
        ends_ref[n * BLOCKS : (n + 1) * BLOCKS, :] = state
    total_ref[...] = join_blocks(ends_ref, rate, steps, False)


def backward_ends_kernel(grad_ref, query_ref, rate_ref, ends_ref, total_ref, source):
    steps = grad_ref.shape[0] // BLOCKS
    rate = rate_ref[...]
    modes = rate.shape[0]
    source[...] = (grad_ref[...] * query_ref[...].astype(F32)).astype(BF16).astype(F32)
    decays = spread_rows(jnp.exp(-rate), 0, modes)
    for n, state in enumerate(run_states(source, decays, steps, True)):
        ends_ref[n * BLOCKS : (n + 1) * BLOCKS, :] = state
    total_ref[...] = join_blocks(ends_ref, rate, steps, True)


def forward_kernel(
    place_ref,
    key_ref,
    value_ref,
    query_ref,
    grad_ref,
    rate_ref,
    gain_ref,
    ends_ref,
    gathered_ref,
    gated_ref,
    query_grad_ref,
    corr_ref,
    product,
    weighted,
    conv,
    carries,
):
    steps = key_ref.shape[0] // BLOCKS
    rate = rate_ref[...]
    modes = rate.shape[0]
    decay = jnp.exp(-rate)
    query = query_ref[...].astype(F32)
    product[...] = (key_ref[...].astype(F32) * value_ref[...].astype(F32)).astype(BF16).astype(F32)
    weighted[...] = (grad_ref[...] * query).astype(BF16).astype(F32)
    block_carries(gathered_ref, ends_ref, rate, place_ref[0], steps, carries, False)
    half = modes // 2
    for first in (0, half):
        decays = spread_rows(decay, first, half)
        gains = spread_rows(gain_ref[...], first, half)

        def body(outer, held, first=first, decays=decays, gains=gains):
            states, sums = held
            for inner in range(UNROLL):
                t = outer * UNROLL + inner
                x = row(product, t, steps)
                w = row(weighted, t, steps)
                states = [d * s + x for d, s in zip(decays, states)]
                sums = [c + w * s for c, s in zip(sums, states)]
                terms = [g * s for g, s in zip(gains, states)]
                if first:
                    terms.append(row(conv, t, steps))
                conv[pl.ds(t, BLOCKS, stride=steps), :] = tree_sum(terms)
            return states, sums

        starts = [carries[n * BLOCKS : (n + 1) * BLOCKS, :] for n in range(first, first + half)]
        zeros = [jnp.zeros((BLOCKS, LANES), F32) for _ in range(half)]
        _, sums = lax.fori_loop(0, steps // UNROLL, body, (starts, zeros))
        for n, total in enumerate(sums):
            corr_ref[first + n : first + n + 1, :] = jnp.sum(total, axis=0, keepdims=True)
    convolved = conv[...]
    gated_ref[...] = (query * convolved).astype(BF16)
    query_grad_ref[...] = (grad_ref[...] * convolved).astype(BF16)


def backward_kernel(
    place_ref,
    grad_ref,
    query_ref,
    key_ref,
    value_ref,
    rate_ref,
    gain_ref,
    ends_ref,
    gathered_ref,
    key_grad_ref,
    value_grad_ref,
    weighted,
    conv,
    carries,
):
    steps = key_ref.shape[0] // BLOCKS
    rate = rate_ref[...]
    modes = rate.shape[0]
    weighted[...] = (grad_ref[...] * query_ref[...].astype(F32)).astype(BF16).astype(F32)
    block_carries(gathered_ref, ends_ref, rate, place_ref[0], steps, carries, True)
    decays = spread_rows(jnp.exp(-rate), 0, modes)
    gains = spread_rows(gain_ref[...], 0, modes)

    def body(outer, states):
        for inner in range(UNROLL):
            t = steps - 1 - (outer * UNROLL + inner)
            x = row(weighted, t, steps)
            states = [d * s + x for d, s in zip(decays, states)]
            conv[pl.ds(t, BLOCKS, stride=steps), :] = tree_sum(
                [g * s for g, s in zip(gains, states)]
            )
        return states

    starts = [carries[n * BLOCKS : (n + 1) * BLOCKS, :] for n in range(modes)]
    lax.fori_loop(0, steps // UNROLL, body, starts)
    grad_product = conv[...]
    key_grad_ref[...] = (grad_product * value_ref[...].astype(F32)).astype(BF16)
    value_grad_ref[...] = (grad_product * key_ref[...].astype(F32)).astype(BF16)


def by_lanes(rows):
    return pl.BlockSpec((rows, LANES), lambda i: (0, i))


def call(kernel, arrays, specs, outs, scratch_rows, flops):
    width = outs[0].shape[1]
    moved = sum(a.size * a.dtype.itemsize for a in list(arrays) + list(outs))
    return pl.pallas_call(
        kernel,
        grid=(width // LANES,),
        in_specs=specs,
        out_specs=[by_lanes(o.shape[0]) for o in outs],
        out_shape=outs,
        scratch_shapes=[pltpu.VMEM((r, LANES), F32) for r in scratch_rows],
        cost_estimate=pl.CostEstimate(flops=flops, bytes_accessed=moved, transcendentals=0),
        compiler_params=pltpu.CompilerParams(vmem_limit_bytes=32 * 2**20),
    )(*arrays)


def per_device(query_in, key_in, value_in, decay_time, residue, out_weight, cotangent):
    decay_rate = 1.0 / decay_time
    norm_factor = jnp.sqrt(-jnp.expm1(-2.0 * decay_rate))
    rate = decay_rate.T
    gain = (norm_factor * residue).T
    seq_count = lax.axis_size("seq")
    place = lax.axis_index("seq").astype(jnp.int32).reshape(1)
    rows, width = query_in.shape
    modes = rate.shape[0]
    work = rows * width * modes
    ends_shape = jax.ShapeDtypeStruct((modes * BLOCKS, width), F32)
    total_shape = jax.ShapeDtypeStruct((modes, width), F32)
    wide = jax.ShapeDtypeStruct((rows, width), BF16)
    big, mode_spec, ends_spec = by_lanes(rows), by_lanes(modes), by_lanes(modes * BLOCKS)
    place_spec = pl.BlockSpec(memory_space=pltpu.SMEM)
    gathered_spec = pl.BlockSpec((seq_count, modes, LANES), lambda i: (0, 0, i))

    all_cotangent = lax.all_gather(cotangent, "chan", axis=1, tiled=True)
    forward_ends, forward_total = call(
        forward_ends_kernel,
        (key_in, value_in, rate),
        [big, big, mode_spec],
        [ends_shape, total_shape],
        [rows],
        2 * work,
    )
    forward_all = lax.all_gather(forward_total, "seq", axis=0)
    grad_gated = lax.dot_general(
        all_cotangent, out_weight, (((1,), (1,)), ((), ())), preferred_element_type=F32
    )
    backward_ends, backward_total = call(
        backward_ends_kernel,
        (grad_gated, query_in, rate),
        [big, big, mode_spec],
        [ends_shape, total_shape],
        [rows],
        2 * work,
    )
    backward_all = lax.all_gather(backward_total, "seq", axis=0)
    gated, query_grad, corr = call(
        forward_kernel,
        (place, key_in, value_in, query_in, grad_gated, rate, gain, forward_ends, forward_all),
        [place_spec, big, big, big, big, mode_spec, mode_spec, ends_spec, gathered_spec],
        [wide, wide, total_shape],
        [rows, rows, rows, modes * BLOCKS],
        6 * work,
    )
    partial_out = jnp.dot(gated, out_weight, preferred_element_type=F32)
    mixed_out = lax.psum_scatter(
        partial_out.astype(BF16), "chan", scatter_dimension=1, tiled=True
    )
    correlation = lax.psum(corr, "seq").T
    key_grad, value_grad = call(
        backward_kernel,
        (place, grad_gated, query_in, key_in, value_in, rate, gain, backward_ends, backward_all),
        [place_spec, big, big, big, big, mode_spec, mode_spec, ends_spec, gathered_spec],
        [wide, wide],
        [rows, rows, modes * BLOCKS],
        4 * work,
    )
    residue_grad = norm_factor * correlation / jnp.sqrt(F32(rows * seq_count))
    return (mixed_out, query_grad, key_grad, value_grad, residue_grad)


def solution(mesh):
    tokens, group = P("seq", "chan"), P("chan", None)
    return jax.shard_map(
        per_device,
        mesh=mesh,
        in_specs=(tokens, tokens, tokens, group, group, group, tokens),
        out_specs=(tokens, tokens, tokens, tokens, group),
        check_vma=False,
    )
```

time: 1610 us -> 332 us (0.21)
  matrix products: 890 us -> 29.6 us
  local copies, waits for them, and re-layouts: 444 us -> 20.6 us
  waiting for transfers between devices: 51.9 us -> 193 us
  blocking collectives: 126 us -> 0 us
  Pallas kernels: 0 us -> 71.5 us
  other arithmetic: 44.5 us -> 2.73 us
  starting transfers between devices: 22.3 us -> 0.2 us
    dot_general x66 -> x2, matrix products: 890 us -> 29.6 us  [the longest x1 15.1 us: per_device(): lax.dot_general(all_cotangent, out_weight, (((1,), (1,)), ((), ())), pref...]
    reshape x18 -> x0, local copies, waits for them, and re-layouts: 147 us -> none  [the longest x16 146 us: spread(): return widened.reshape(lead + (channel_count * mode_count,))]
    while x56 -> x0, local copies, waits for them, and re-layouts: 119 us -> none
    all_gather x1 -> x3, waiting for transfers between devices: 0.02 us -> 116 us  [the longest x1 61.3 us: per_device(): backward_all = lax.all_gather(backward_total, 'seq', axis=0)]
    psum x0 -> x1, waiting for transfers between devices: none -> 76.3 us  [per_device(): correlation = lax.psum(corr, 'seq').T]
    pallas_call x0 -> x4, Pallas kernels: none -> 71.5 us  [call(): pl.pallas_call(kernel, grid=(width // LANES,), in_specs=specs, out_specs=...]
    all_gather x1 -> x0, blocking collectives: 67.6 us -> none  [per_device(): lax.all_gather(scale_part * correlation, 'seq', axis=0, tiled=True)]
    all_to_all x1 -> x0, blocking collectives: 58 us -> none  [per_device(): lax.all_to_all(conv_full.astype(jnp.bfloat16), 'seq', split_axis=0, conca...]
  transfers between devices with their start and end apart: 5 -> 5, of which waited for: 2 -> 4; matrix products, arithmetic and copies ran while one was open for 5% -> 10% of each run, Pallas kernels for 0% -> 12%
where the time goes in v1:
time: 332 us; the launch traced here: 331 us
  waiting for transfers between devices  193 us (58%)
  Pallas kernels  71.5 us (22%)
  matrix products  29.6 us (9%)
  local copies, waits for them, and re-layouts  20.6 us (6%)
  between operations  13.8 us (4%)
    psum x1, waiting for transfers between devices, per_device(): correlation = lax.psum(corr, 'seq').T  76.3 us
    pallas_call x4, Pallas kernels, call(): pl.pallas_call(kernel, grid=(width // LANES,), in_specs=specs, out_specs=...  71.5 us
    all_gather x1, waiting for transfers between devices, per_device(): backward_all = lax.all_gather(backward_total, 'seq', axis=0)  61.3 us
    all_gather x1, waiting for transfers between devices, per_device(): forward_all = lax.all_gather(forward_total, 'seq', axis=0)  50.2 us
    unnamed x28, local copies, waits for them, and re-layouts  20.6 us
    dot_general x1, matrix products, per_device(): lax.dot_general(all_cotangent, out_weight, (((1,), (1,)), ((), ())), pref...  15.1 us
    dot_general x1, matrix products, per_device(): partial_out = jnp.dot(gated, out_weight, preferred_element_type=F32)  14.5 us
  transfers between devices with their start and end apart: 5, of which 4 were waited for; matrix products, arithmetic and copies ran while one was open for 10% of the time, Pallas kernels for 12%

profile of v1, /device:TPU:0, one launch (start us, length us, event | category | flops | bytes accessed | tf_op | source)
XLA Modules:
  0.0 331.1 jit_solution(14607797822500628877)
XLA Ops:
  7.9 1.1 multiply_bitcast_fusion
  9.0 1.6 copy-done.4
  10.6 1.6 copy-done.7
  12.2 9.6 %shard_map.110 = (f32[128,2048]{1,0:T(8,128)S(1)}, f32[16,2048]{1,0:T(8,128)}) custom-call(bf16[512,2048]{1,0:T(8,128)(2,1)S(1)} %copy-done.4, bf16[512,2048]{1,0:T(8,128)(2,1)S(1)} %copy-done.7, f32[16,2048]{1,0:T(8,128)S(1)} %get-tuple-element.24.rate_ref), custom_call_target="tpu_custom_call" | custom-call | flops 33554432 | bytes 5505024 | tf_op jit(solution)/shard_map/pallas_call | solution.py:194
  21.9 4.0 %all-gather.6.cloned.1.call-done = bf16[512,4096]{1,0:T(8,128)(2,1)} async-done(((bf16[512,2048]{1,0:T(8,128)(2,1)}), bf16[512,4096]{1,0:T(8,128)(2,1)}) %all-gather.6.cloned.1.call-update) | async-done | bytes 4194320 | tf_op jit(solution)/shard_map/all_gather | solution.py:223
  25.9 15.1 %fusion.1.grad_ref = f32[512,2048]{1,0:T(8,128)} fusion(bf16[512,4096]{1,0:T(8,128)(2,1)} %all-gather.6.cloned.1.call-done, bf16[2048,4096]{1,0:T(8,128)(2,1)} %param.12), kind=kOutput, calls=%fused_computation.6 | convolution fusion | flops 8589934592 | bytes 25165824 | tf_op jit(solution)/shard_map/dot_general | solution.py:233
  41.0 50.2 %all-gather.8.cloned.1.call-done = f32[256,2048]{1,0:T(8,128)} async-done(((f32[16,2048]{1,0:T(8,128)}), f32[256,2048]{1,0:T(8,128)}) %all-gather.8.cloned.1.call-update) | async-done | bytes 2097168 | tf_op jit(solution)/shard_map/all_gather | solution.py:232
  91.2 2.2 copy-done
  93.4 1.6 copy-done.5
  95.0 1.6 copy-done.8
  96.6 1.6 copy-done.11
  98.2 32.0 %shard_map.111 = (bf16[512,2048]{1,0:T(8,128)(2,1)S(1)}, bf16[512,2048]{1,0:T(8,128)(2,1)}, f32[16,2048]{1,0:T(8,128)}) custom-call(s32[1]{0:T(128)} %bitcast.place_ref, bf16[512,2048]{1,0:T(8,128)(2,1)S(1)} %copy-done.5, bf16[512,2048]{1,0:T(8,128)(2,1)S(1)} %copy-done.8, bf16[512,2048]{1,0:T(8,128)(2,1)S(1)} %copy-done.3, f32[512,2048]{1,0:T(8,128)S(1)} %copy-done, ...), custom_call_target="tpu_custom_call" | custom-call | flops 100663296 | bytes 18219012 | tf_op jit(solution)/shard_map/pallas_call | solution.py:194
  130.2 1.3 copy-done.12
  131.6 2.2 copy-done.1
  133.8 9.9 %shard_map.112 = (f32[128,2048]{1,0:T(8,128)S(1)}, f32[16,2048]{1,0:T(8,128)}) custom-call(f32[512,2048]{1,0:T(8,128)S(1)} %copy-done.1, bf16[512,2048]{1,0:T(8,128)(2,1)S(1)} %copy-done.3, f32[16,2048]{1,0:T(8,128)S(1)} %get-tuple-element.24.rate_ref), custom_call_target="tpu_custom_call" | custom-call | flops 33554432 | bytes 7602176 | tf_op jit(solution)/shard_map/pallas_call | solution.py:194
  143.7 14.5 %convolution_convert_fusion = bf16[512,4096]{1,0:T(8,128)(2,1)} fusion(bf16[512,2048]{1,0:T(8,128)(2,1)} %copy-done.12, bf16[2048,4096]{1,0:T(8,128)(2,1)} %param.12), kind=kOutput, calls=%fused_computation | convolution fusion | flops 8592031744 | bytes 23068672 | tf_op jit(solution)/shard_map/dot_general | solution.py:253
  158.2 76.3 %all-reduce.2.cloned.1.call-done = f32[2048,16]{0,1:T(8,128)} async-done(((f32[2048,16]{0,1:T(8,128)}), f32[2048,16]{0,1:T(8,128)}) %all-reduce.2.cloned.1.call-update) | async-done | bytes 131088 | tf_op jit(solution)/shard_map/psum | solution.py:257
  234.6 1.7 multiply_multiply_fusion
  236.2 61.3 %all-gather.10.cloned.1.call-done = f32[256,2048]{1,0:T(8,128)} async-done(((f32[16,2048]{1,0:T(8,128)}), f32[256,2048]{1,0:T(8,128)}) %all-gather.10.cloned.1.call-update) | async-done | bytes 2097168 | tf_op jit(solution)/shard_map/all_gather | solution.py:244
  297.5 2.2 copy-done.2
  299.7 1.6 copy-done.6
  301.3 1.6 copy-done.9
  302.9 1.6 copy-done.10
  304.5 20.0 %shard_map.113 = (bf16[512,2048]{1,0:T(8,128)(2,1)}, bf16[512,2048]{1,0:T(8,128)(2,1)}) custom-call(s32[1]{0:T(128)} %bitcast.place_ref, f32[512,2048]{1,0:T(8,128)S(1)} %copy-done.2, bf16[512,2048]{1,0:T(8,128)(2,1)S(1)} %copy-done.3, bf16[512,2048]{1,0:T(8,128)(2,1)S(1)} %copy-done.6, bf16[512,2048]{1,0:T(8,128)(2,1)S(1)} %copy-done.9, ...), custom_call_target="tpu_custom_call" | custom-call | flops 67108864 | bytes 18087940 | tf_op jit(solution)/shard_map/pallas_call | solution.py:194
  (27 shorter events, 1.0 us)
Async XLA Ops:
  7.2 18.8 %all-gather.6.cloned.1.call-start = ((), (), s32[]{:S(2)}) async-start(), calls=%async_computation.1 | async-start | bytes 6291456 | tf_op jit(solution)/shard_map/all_gather | solution.py:223
  7.9 83.3 %all-gather.8.cloned.1.call-start = ((), (), s32[]{:S(2)}) async-start(), calls=%async_computation.4 | async-start | bytes 2228224 | tf_op jit(solution)/shard_map/all_gather | solution.py:232
  9.0 1.6 copy-start.4
  10.6 1.6 copy-start.7
  21.8 212.7 %all-reduce.2.cloned.1.call-start = ((), (), s32[]{:S(2)}) async-start(), calls=%async_computation.3 | async-start | bytes 262144 | tf_op jit(solution)/shard_map/psum | solution.py:257
  21.9 69.3 %copy-start.3 = (bf16[512,2048]{1,0:T(8,128)(2,1)S(1)}, bf16[512,2048]{1,0:T(8,128)(2,1)}, u32[]{:S(2)}) copy-start(bf16[512,2048]{1,0:T(8,128)(2,1)} %query_ref.5) | copy-start | bytes 6291460
  91.2 2.2 copy-start
  93.4 1.6 copy-start.5
  95.0 1.6 copy-start.8
  96.6 1.6 copy-start.11
  130.2 1.3 copy-start.12
  131.5 166.0 %all-gather.10.cloned.1.call-start = ((), (), s32[]{:S(2)}) async-start(), calls=%async_computation.5 | async-start | bytes 2228224 | tf_op jit(solution)/shard_map/all_gather | solution.py:244
  131.6 2.2 copy-start.1
  143.7 180.9 %reduce-scatter.2.cloned.1.call-start = ((), (), s32[]{:S(2)}) async-start(), calls=%async_computation.2 | async-start | bytes 6291456 | tf_op jit(solution)/shard_map/reduce_scatter | solution.py:254
  158.2 76.3 %copy-start.13 = (f32[2048,16]{0,1:T(8,128)S(1)}, f32[2048,16]{0,1:T(8,128)}, u32[]{:S(2)}) copy-start(f32[2048,16]{0,1:T(8,128)} %param.10) | copy-start | bytes 393220
  297.5 2.2 copy-start.2
  299.7 1.6 copy-start.6
  301.3 1.6 copy-start.9
  302.9 1.6 copy-start.10
Sparse Core Ops, SparseCore 0:
  9.5 16.3 all-gather.5
  29.3 61.8 all-gather.7
  131.7 102.8 all-reduce.1
  237.8 59.7 all-gather.9
  300.2 10.6 reduce-scatter.1

commit v2 on v1

v2 whole, which is shorter than its diff:
```python
import functools

import jax
import jax.numpy as jnp
from jax import lax
from jax.experimental import pallas as pl
from jax.experimental.pallas import tpu as pltpu
from jax.sharding import PartitionSpec as P

LANES = 128
BLOCKS = 8
F32 = jnp.float32
BF16 = jnp.bfloat16


def tree_sum(terms):
    while len(terms) > 1:
        pairs = [terms[i] + terms[i + 1] for i in range(0, len(terms) - 1, 2)]
        terms = pairs + terms[len(terms) - len(terms) % 2 :]
    return terms[0]


def swap_rows(tiles):
    rows = lax.broadcasted_iota(jnp.int32, (BLOCKS, LANES), 0)
    for bit in (1, 2, 4):
        low = (rows & bit) == 0
        swapped = list(tiles)
        for i in range(BLOCKS):
            if i & bit == 0:
                a, b = tiles[i], tiles[i | bit]
                swapped[i] = jnp.where(low, a, pltpu.roll(b, bit, axis=0))
                swapped[i | bit] = jnp.where(low, pltpu.roll(a, BLOCKS - bit, axis=0), b)
        tiles = swapped
    return tiles


def block_tile(b, group, steps):
    return pl.ds(pl.multiple_of(b * steps + group * BLOCKS, BLOCKS), BLOCKS)


def load_steps(ref, group, steps):
    return swap_rows([ref[block_tile(b, group, steps), :] for b in range(BLOCKS)])


def store_steps(ref, group, steps, tiles):
    for b, tile in enumerate(swap_rows(tiles)):
        ref[block_tile(b, group, steps), :] = tile


def step_tile(group, inner):
    return pl.ds(pl.multiple_of((group * BLOCKS + inner) * BLOCKS, BLOCKS), BLOCKS)


def spread_rows(rate, first, count):
    return [
        jnp.broadcast_to(rate[n : n + 1, :], (BLOCKS, LANES)) for n in range(first, first + count)
    ]


def block_rows(ends, b, modes):
    return ends[pl.ds(b, modes, stride=BLOCKS), :]


def join_blocks(ends, rate, steps, backward):
    modes = rate.shape[0]
    step_decay = jnp.exp(-rate * float(steps))
    total = jnp.zeros((modes, LANES), F32)
    for b in reversed(range(BLOCKS)) if backward else range(BLOCKS):
        total = total * step_decay + block_rows(ends, b, modes)
    return total


def fill_carries(entering, ends, rate, steps, carries, backward):
    modes = rate.shape[0]
    step_decay = jnp.exp(-rate * float(steps))
    run = entering
    for b in reversed(range(BLOCKS)) if backward else range(BLOCKS):
        carries[pl.ds(b, modes, stride=BLOCKS), :] = run
        run = run * step_decay + block_rows(ends, b, modes)


def take(ref, n):
    return ref[n * BLOCKS : (n + 1) * BLOCKS, :]


def rounded_product(a, b):
    return (a.astype(F32) * b.astype(F32)).astype(BF16).astype(F32)


def zero_rows(count):
    return [jnp.zeros((BLOCKS, LANES), F32) for _ in range(count)]


def forward_local_kernel(
    key_ref, value_ref, rate_ref, gain_ref, conv_ref, ends_ref, total_ref, product
):
    steps = key_ref.shape[0] // BLOCKS
    rate = rate_ref[...]
    modes = rate.shape[0]
    product[...] = rounded_product(key_ref[...], value_ref[...])
    decays = spread_rows(jnp.exp(-rate), 0, modes)
    gains = spread_rows(gain_ref[...], 0, modes)

    def body(group, states):
        results = []
        for x in load_steps(product, group, steps):
            states = [d * s + x for d, s in zip(decays, states)]
            results.append(tree_sum([g * s for g, s in zip(gains, states)]))
        store_steps(conv_ref, group, steps, results)
        return states

    for n, state in enumerate(lax.fori_loop(0, steps // BLOCKS, body, zero_rows(modes))):
        ends_ref[n * BLOCKS : (n + 1) * BLOCKS, :] = state
    total_ref[0, 0] = join_blocks(ends_ref, rate, steps, False)


def backward_local_kernel(
    key_ref,
    value_ref,
    query_ref,
    grad_ref,
    rate_ref,
    gain_ref,
    forward_ends_ref,
    conv_ref,
    ends_ref,
    summary_ref,
    product,
    weighted,
    product_steps,
    weighted_steps,
    part,
    sums_ref,
):
    steps = key_ref.shape[0] // BLOCKS
    rate = rate_ref[...]
    modes = rate.shape[0]
    product[...] = rounded_product(key_ref[...], value_ref[...])
    weighted[...] = (grad_ref[...] * query_ref[...].astype(F32)).astype(BF16).astype(F32)
    decay = jnp.exp(-rate)
    groups = steps // BLOCKS

    def reorder(group, carry):
        for source, target in ((product, product_steps), (weighted, weighted_steps)):
            for inner, tile in enumerate(load_steps(source, group, steps)):
                target[step_tile(group, inner), :] = tile
        return carry

    lax.fori_loop(0, groups, reorder, 0)
    half = modes // 2
    for first in (0, half):
        decays = spread_rows(decay, first, half)
        gains = spread_rows(gain_ref[...], first, half)

        def body(outer, held, first=first, decays=decays, gains=gains):
            states, sums = held
            group = groups - 1 - outer
            results = []
            for inner in reversed(range(BLOCKS)):
                x = product_steps[step_tile(group, inner), :]
                w = weighted_steps[step_tile(group, inner), :]
                states = [d * s + w for d, s in zip(decays, states)]
                sums = [c + x * s for c, s in zip(sums, states)]
                terms = [g * s for g, s in zip(gains, states)]
                if first:
                    results.insert(0, tree_sum(terms + [part[step_tile(group, inner), :]]))
                else:
                    part[step_tile(group, inner), :] = tree_sum(terms)
            if first:
                store_steps(conv_ref, group, steps, results)
            return states, sums

        states, sums = lax.fori_loop(
            0, groups, body, (zero_rows(half), zero_rows(half))
        )
        for n in range(half):
            ends_ref[(first + n) * BLOCKS : (first + n + 1) * BLOCKS, :] = states[n]
            sums_ref[(first + n) * BLOCKS : (first + n + 1) * BLOCKS, :] = sums[n]
    step_decay = jnp.exp(-rate * float(steps))
    run = jnp.zeros((modes, LANES), F32)
    total = jnp.zeros((modes, LANES), F32)
    for b in reversed(range(BLOCKS)):
        total = total + block_rows(sums_ref, b, modes)
        total = total + decay * block_rows(forward_ends_ref, b, modes) * run
        run = run * step_decay + block_rows(ends_ref, b, modes)
    summary_ref[0, 0] = run
    summary_ref[0, 1] = total


def forward_join_kernel(row_count, held, rate_ref, answer):
    rate = rate_ref[...]
    device_decay = jnp.exp(-rate * float(row_count))
    run = jnp.zeros_like(rate)
    for e in range(held.shape[0]):
        answer[e, 0] = run
        run = run * device_decay + held[e, 0]


def backward_join_kernel(row_count, held, forward_held, rate_ref, answer):
    rate = rate_ref[...]
    count = held.shape[0]
    decay = jnp.exp(-rate)
    device_decay = jnp.exp(-rate * float(row_count))
    run = jnp.zeros_like(rate)
    total = jnp.zeros_like(rate)
    for e in reversed(range(count)):
        answer[e, 0] = run
        total = total + held[e, 1] + decay * forward_held[e, 0] * run
        run = run * device_decay + held[e, 0]
    for e in range(count):
        answer[e, 1] = total


def join(kernel, row_count, arrays, out):
    return pl.pallas_call(
        functools.partial(kernel, row_count),
        out_shape=jax.ShapeDtypeStruct(out.shape, F32),
        in_specs=[pl.BlockSpec(memory_space=pltpu.VMEM)] * len(arrays),
        out_specs=pl.BlockSpec(memory_space=pltpu.VMEM),
    )(*arrays)


def trade(chunks):
    return lax.all_to_all(chunks, "seq", split_axis=0, concat_axis=0, tiled=True)


def forward_kernel(
    query_ref,
    grad_ref,
    conv_ref,
    rate_ref,
    gain_ref,
    ends_ref,
    carry_ref,
    gated_ref,
    query_grad_ref,
    conv,
    carries,
):
    steps = query_ref.shape[0] // BLOCKS
    rate = rate_ref[...]
    modes = rate.shape[0]
    decay = jnp.exp(-rate)
    fill_carries(carry_ref[0, 0], ends_ref, rate, steps, carries, False)
    decays = spread_rows(decay, 0, modes)
    firsts = spread_rows(decay * gain_ref[...], 0, modes)

    def body(group, states):
        results = []
        for _ in range(BLOCKS):
            results.append(tree_sum(states))
            states = [d * s for d, s in zip(decays, states)]
        store_steps(conv, group, steps, results)
        return states

    starts = [g * take(carries, n) for n, g in enumerate(firsts)]
    lax.fori_loop(0, steps // BLOCKS, body, starts)
    convolved = conv_ref[...] + conv[...]
    gated_ref[...] = (query_ref[...].astype(F32) * convolved).astype(BF16)
    query_grad_ref[...] = (grad_ref[...] * convolved).astype(BF16)


def backward_kernel(
    key_ref,
    value_ref,
    conv_ref,
    rate_ref,
    gain_ref,
    ends_ref,
    carry_ref,
    key_grad_ref,
    value_grad_ref,
    conv,
    carries,
):
    steps = key_ref.shape[0] // BLOCKS
    rate = rate_ref[...]
    modes = rate.shape[0]
    decay = jnp.exp(-rate)
    fill_carries(carry_ref[0, 0], ends_ref, rate, steps, carries, True)
    decays = spread_rows(decay, 0, modes)
    firsts = spread_rows(decay * gain_ref[...], 0, modes)

    def body(outer, states):
        results = []
        for _ in range(BLOCKS):
            results.insert(0, tree_sum(states))
            states = [d * s for d, s in zip(decays, states)]
        store_steps(conv, steps // BLOCKS - 1 - outer, steps, results)
        return states

    starts = [g * take(carries, n) for n, g in enumerate(firsts)]
    lax.fori_loop(0, steps // BLOCKS, body, starts)
    grad_product = conv_ref[...] + conv[...]
    key_grad_ref[...] = (grad_product * value_ref[...].astype(F32)).astype(BF16)
    value_grad_ref[...] = (grad_product * key_ref[...].astype(F32)).astype(BF16)


def by_lanes(rows):
    return pl.BlockSpec((rows, LANES), lambda i: (0, i))


def call(kernel, arrays, specs, outs, out_specs, scratch_rows, flops):
    groups = arrays[0].shape[1] // LANES
    moved = sum(a.size * a.dtype.itemsize for a in list(arrays) + list(outs))
    return pl.pallas_call(
        kernel,
        grid=(groups,),
        in_specs=specs,
        out_specs=out_specs,
        out_shape=outs,
        scratch_shapes=[pltpu.VMEM((r, LANES), F32) for r in scratch_rows],
        cost_estimate=pl.CostEstimate(flops=flops, bytes_accessed=moved, transcendentals=0),
        compiler_params=pltpu.CompilerParams(vmem_limit_bytes=56 * 2**20),
    )(*arrays)


def to_chunks(grouped, count):
    groups, kinds, modes, lanes = grouped.shape
    cuts = count // groups
    cut = grouped.reshape(groups, kinds, cuts, modes // cuts, lanes)
    return cut.transpose(0, 2, 1, 3, 4).reshape(count, kinds, modes // cuts, lanes)


def from_chunks(chunks, groups):
    count, kinds, part, lanes = chunks.shape
    cuts = count // groups
    cut = chunks.reshape(groups, cuts, kinds, part, lanes)
    return cut.transpose(0, 2, 1, 3, 4).reshape(groups, kinds, cuts * part, lanes)


def per_device(query_in, key_in, value_in, decay_time, residue, out_weight, cotangent):
    decay_rate = 1.0 / decay_time
    norm_factor = jnp.sqrt(-jnp.expm1(-2.0 * decay_rate))
    rate = decay_rate.T
    gain = (norm_factor * residue).T
    seq_count = lax.axis_size("seq")
    rows, width = query_in.shape
    modes = rate.shape[0]
    groups = width // LANES
    work = rows * width * modes
    ends_shape = jax.ShapeDtypeStruct((modes * BLOCKS, width), F32)
    total_shape = jax.ShapeDtypeStruct((groups, 1, modes, LANES), F32)
    summary_shape = jax.ShapeDtypeStruct((groups, 2, modes, LANES), F32)
    narrow = jax.ShapeDtypeStruct((rows, width), BF16)
    wide = jax.ShapeDtypeStruct((rows, width), F32)
    big, mode_spec, ends_spec = by_lanes(rows), by_lanes(modes), by_lanes(modes * BLOCKS)
    total_spec = pl.BlockSpec((1, 1, modes, LANES), lambda i: (i, 0, 0, 0))
    summary_spec = pl.BlockSpec((1, 2, modes, LANES), lambda i: (i, 0, 0, 0))
    rate_groups = rate.reshape(modes, groups, LANES).transpose(1, 0, 2)[:, None]
    own_rate = lax.dynamic_index_in_dim(
        to_chunks(rate_groups, seq_count)[:, 0], lax.axis_index("seq"), 0, keepdims=False
    )

    all_cotangent = lax.all_gather(cotangent, "chan", axis=1, tiled=True)
    forward_local, forward_ends, forward_total = call(
        forward_local_kernel,
        (key_in, value_in, rate, gain),
        [big, big, mode_spec, mode_spec],
        [wide, ends_shape, total_shape],
        [big, ends_spec, total_spec],
        [rows],
        4 * work,
    )
    forward_held = trade(to_chunks(forward_total, seq_count))
    forward_answer = join(
        forward_join_kernel, rows, (forward_held, own_rate), forward_held
    )
    forward_carry = from_chunks(trade(forward_answer), groups)
    grad_gated = lax.dot_general(
        all_cotangent, out_weight, (((1,), (1,)), ((), ())), preferred_element_type=F32
    )
    backward_local, backward_ends, summary = call(
        backward_local_kernel,
        (key_in, value_in, query_in, grad_gated, rate, gain, forward_ends),
        [big, big, big, big, mode_spec, mode_spec, ends_spec],
        [wide, ends_shape, summary_shape],
        [big, ends_spec, summary_spec],
        [rows] * 5 + [modes * BLOCKS],
        6 * work,
    )
    backward_held = trade(to_chunks(summary, seq_count))
    backward_answer = join(
        backward_join_kernel, rows, (backward_held, forward_held, own_rate), backward_held
    )
    joined = from_chunks(trade(backward_answer), groups)
    gated, query_grad = call(
        forward_kernel,
        (query_in, grad_gated, forward_local, rate, gain, forward_ends, forward_carry),
        [big, big, big, mode_spec, mode_spec, ends_spec, total_spec],
        [narrow, narrow],
        [big, big],
        [rows, modes * BLOCKS],
        2 * work,
    )
    partial_out = jnp.dot(gated, out_weight, preferred_element_type=F32)
    mixed_out = lax.psum_scatter(
        partial_out.astype(BF16), "chan", scatter_dimension=1, tiled=True
    )
    key_grad, value_grad = call(
        backward_kernel,
        (key_in, value_in, backward_local, rate, gain, backward_ends, joined),
        [big, big, big, mode_spec, mode_spec, ends_spec, summary_spec],
        [narrow, narrow],
        [big, big],
        [rows, modes * BLOCKS],
        2 * work,
    )
    correlation = joined[:, 1].transpose(0, 2, 1).reshape(width, modes)
    residue_grad = norm_factor * correlation / jnp.sqrt(F32(rows * seq_count))
    return (mixed_out, query_grad, key_grad, value_grad, residue_grad)


def solution(mesh):
    tokens, group = P("seq", "chan"), P("chan", None)
    return jax.shard_map(
        per_device,
        mesh=mesh,
        in_specs=(tokens, tokens, tokens, group, group, group, tokens),
        out_specs=(tokens, tokens, tokens, tokens, group),
        check_vma=False,
    )
```

time: 332 us -> 169 us (0.51)
  waiting for transfers between devices: 193 us -> 7.87 us
  blocking collectives: 0 us -> 28.2 us
  local copies, waits for them, and re-layouts: 20.6 us -> 1.95 us
  starting transfers between devices: 0.2 us -> 12 us
    all_gather x2 -> x0, waiting for transfers between devices: 111 us -> none  [the longest x1 61.3 us: per_device(): backward_all = lax.all_gather(backward_total, 'seq', axis=0)]
    psum x1 -> x0, waiting for transfers between devices: 76.3 us -> none  [per_device(): correlation = lax.psum(corr, 'seq').T]
    all_to_all x0 -> x2, blocking collectives: none -> 28.2 us  [trade(): lax.all_to_all(chunks, 'seq', split_axis=0, concat_axis=0, tiled=True)]
    unnamed x28 -> x9, local copies, waits for them, and re-layouts: 20.6 us -> 1.33 us
    all_to_all x0 -> x2, starting transfers between devices: none -> 11.9 us  [trade(): lax.all_to_all(chunks, 'seq', split_axis=0, concat_axis=0, tiled=True)]
    all_to_all x0 -> x2, waiting for transfers between devices: none -> 7.15 us  [trade(): lax.all_to_all(chunks, 'seq', split_axis=0, concat_axis=0, tiled=True)]
    all_gather x1, waiting for transfers between devices: 4.04 us -> 0.02 us  [per_device(): all_cotangent = lax.all_gather(cotangent, 'chan', axis=1, tiled=True)]
    pallas_call x4 -> x6, Pallas kernels: 71.5 us -> 71.5 us  [the longest x4 68.1 us: call(): pl.pallas_call(kernel, grid=(groups,), in_specs=specs, out_specs=out_spec...]
  transfers between devices with their start and end apart: 5 -> 4, of which waited for: 4 -> 1; matrix products, arithmetic and copies ran while one was open for 10% -> 11% of each run, Pallas kernels for 12% -> 34%
where the time goes in v2:
time: 169 us; the launch traced here: 168 us
  Pallas kernels  71.5 us (42%)
  matrix products  29.5 us (17%)
  blocking collectives  28.2 us (17%)
  between operations  14.1 us (8%)
  starting transfers between devices  12 us (7%)
  waiting for transfers between devices  7.87 us (5%)
  other arithmetic  2.5 us (1%)
  local copies, waits for them, and re-layouts  1.95 us (1%)
    pallas_call x4, Pallas kernels, call(): pl.pallas_call(kernel, grid=(groups,), in_specs=specs, out_specs=out_spec...  68.1 us
    all_to_all x2, blocking collectives, trade(): lax.all_to_all(chunks, 'seq', split_axis=0, concat_axis=0, tiled=True)  28.2 us
    dot_general x1, matrix products, per_device(): lax.dot_general(all_cotangent, out_weight, (((1,), (1,)), ((), ())), pref...  15.1 us
    dot_general x1, matrix products, per_device(): partial_out = jnp.dot(gated, out_weight, preferred_element_type=F32)  14.4 us
    all_to_all x2, starting transfers between devices, trade(): lax.all_to_all(chunks, 'seq', split_axis=0, concat_axis=0, tiled=True)  11.9 us
    all_to_all x2, waiting for transfers between devices, trade(): lax.all_to_all(chunks, 'seq', split_axis=0, concat_axis=0, tiled=True)  7.15 us
    pallas_call x2, Pallas kernels, join(): pl.pallas_call(functools.partial(kernel, row_count), out_shape=jax.ShapeD...  3.38 us
  transfers between devices with their start and end apart: 4, of which 1 were waited for; matrix products, arithmetic and copies ran while one was open for 11% of the time, Pallas kernels for 34%

profile of v2, /device:TPU:0, one launch (start us, length us, event | category | flops | bytes accessed | tf_op | source)
XLA Modules:
  0.0 167.5 jit_solution(5546059671401358891)
XLA Ops:
  7.2 0.0 all-gather.2.cloned.1.call-start
  7.2 0.7 all-gather.2.cloned.1.call-update
  7.9 1.7 %fusion.1 = (f32[2,8,16,128]{3,1,2,0:T(8,128)S(1)}, f32[16,2048]{1,0:T(8,128)}, f32[16,2048]{1,0:T(8,128)}) fusion(f32[2048,16]{0,1:T(8,128)} %param.10, f32[2048,16]{0,1:T(8,128)} %param.11), kind=kLoop, calls=%fused_computation.8 | loop fusion | flops 131072 | bytes 655360
  9.6 16.8 %shard_map.110 = (f32[512,2048]{1,0:T(8,128)}, f32[128,2048]{1,0:T(8,128)}, f32[16,1,16,128]{3,2,1,0:T(8,128)}) custom-call(bf16[512,2048]{1,0:T(8,128)(2,1)} %key_ref.5, bf16[512,2048]{1,0:T(8,128)(2,1)} %value_ref.5, f32[16,2048]{1,0:T(8,128)} %get-tuple-element.27.rate_ref, f32[16,2048]{1,0:T(8,128)} %get-tuple-element.26.gain_ref), custom_call_target="tpu_custom_call" | custom-call | flops 67108864 | bytes 9830400 | tf_op jit(solution)/shard_map/pallas_call | solution.py:306
  26.5 8.4 %all-to-all-start = ((f32[16,1,16,128]{3,2,1,0:T(8,128)}), f32[16,1,16,128]{3,2,1,0:T(8,128)S(1)}, u32[]{:S(2)}, u32[]{:S(2)}) async-start(f32[16,1,16,128]{3,2,1,0:T(8,128)} %get-tuple-element.17), calls=%async_computation | async-start | bytes 262144 | tf_op jit(solution)/shard_map/all_to_all | solution.py:224
  34.9 0.6 constant_dynamic-slice_fusion
  35.5 7.1 %all-to-all-done.held.forward_held = f32[16,1,16,128]{3,2,1,0:T(8,128)S(1)} async-done(((f32[16,1,16,128]{3,2,1,0:T(8,128)}), f32[16,1,16,128]{3,2,1,0:T(8,128)S(1)}, u32[]{:S(2)}, u32[]{:S(2)}) %all-to-all-start) | async-done | bytes 131104 | tf_op jit(solution)/shard_map/all_to_all | solution.py:224
  42.6 0.6 copy-done.1
  43.3 1.6 shard_map.111
  44.9 3.5 %all-to-all-start.1 = ((f32[16,1,16,128]{3,2,1,0:T(8,128)}), f32[16,1,16,128]{3,2,1,0:T(8,128)S(1)}, u32[]{:S(2)}, u32[]{:S(2)}) async-start(f32[16,1,16,128]{3,2,1,0:T(8,128)} %shard_map.111), calls=%async_computation.1 | async-start | bytes 262144 | tf_op jit(solution)/shard_map/all_to_all | solution.py:224
  48.4 0.0 reduce-scatter.2.cloned.1.call-start
  48.5 0.0 all-gather.2.cloned.1.call-done
  48.5 15.1 %fusion.3.grad_ref = f32[512,2048]{1,0:T(8,128)} fusion(bf16[512,4096]{1,0:T(8,128)(2,1)} %all-gather.2.cloned.1.call-done, bf16[2048,4096]{1,0:T(8,128)(2,1)} %param.12), kind=kOutput, calls=%fused_computation.10 | convolution fusion | flops 8589934592 | bytes 25165824 | tf_op jit(solution)/shard_map/dot_general | solution.py:370
  63.6 0.0 all-to-all-done.1.carry_ref
  63.6 0.7 copy-done.2
  64.2 14.8 %shard_map.112 = (bf16[512,2048]{1,0:T(8,128)(2,1)}, bf16[512,2048]{1,0:T(8,128)(2,1)}) custom-call(bf16[512,2048]{1,0:T(8,128)(2,1)} %query_ref.3, f32[512,2048]{1,0:T(8,128)} %fusion.3.grad_ref, f32[512,2048]{1,0:T(8,128)} %get-tuple-element.15.conv_ref, f32[16,2048]{1,0:T(8,128)} %get-tuple-element.27.rate_ref, f32[16,2048]{1,0:T(8,128)} %get-tuple-element.26.gain_ref, ...), custom_call_target="tpu_custom_call" | custom-call | flops 33554432 | bytes 16121856 | tf_op jit(solution)/shard_map/pallas_call | solution.py:306
  79.0 14.4 %convolution_convert_fusion = bf16[512,4096]{1,0:T(8,128)(2,1)} fusion(bf16[512,2048]{1,0:T(8,128)(2,1)} %get-tuple-element.18, bf16[2048,4096]{1,0:T(8,128)(2,1)} %param.12), kind=kOutput, calls=%fused_computation | convolution fusion | flops 8592031744 | bytes 23068672 | tf_op jit(solution)/shard_map/dot_general | solution.py:396
  93.4 0.0 reduce-scatter.2.cloned.1.call-update
  93.5 22.0 %shard_map.113 = (f32[512,2048]{1,0:T(8,128)}, f32[128,2048]{1,0:T(8,128)}, f32[16,2,16,128]{3,2,1,0:T(8,128)}) custom-call(bf16[512,2048]{1,0:T(8,128)(2,1)} %key_ref.5, bf16[512,2048]{1,0:T(8,128)(2,1)} %value_ref.5, bf16[512,2048]{1,0:T(8,128)(2,1)} %query_ref.3, f32[512,2048]{1,0:T(8,128)} %fusion.3.grad_ref, f32[16,2048]{1,0:T(8,128)} %get-tuple-element.27.rate_ref, ...), custom_call_target="tpu_custom_call" | custom-call | flops 100663296 | bytes 17301504 | tf_op jit(solution)/shard_map/pallas_call | solution.py:306
  115.5 15.5 %all_to_all.20.held = f32[16,2,16,128]{3,2,1,0:T(8,128)} all-to-all(f32[16,2,16,128]{3,2,1,0:T(8,128)} %get-tuple-element.22), channel_id=1, replica_groups=mesh['seq'=16,'chan'=2] {'seq'}, dimensions={0} | all-to-all | bytes 524288 | tf_op jit(solution)/shard_map/all_to_all | solution.py:224
  130.9 1.8 %shard_map.114 = f32[16,2,16,128]{3,2,1,0:T(8,128)} custom-call(f32[16,2,16,128]{3,2,1,0:T(8,128)} %all_to_all.20.held, f32[16,1,16,128]{3,2,1,0:T(8,128)} %copy-done.1, f32[16,128]{1,0:T(8,128)} %bitcast.24), custom_call_target="tpu_custom_call" | custom-call | tf_op jit(solution)/shard_map/pallas_call | solution.py:215
  132.7 12.7 %all_to_all.21.carry_ref = f32[16,2,16,128]{3,2,1,0:T(8,128)} all-to-all(f32[16,2,16,128]{3,2,1,0:T(8,128)} %shard_map.114), channel_id=1, replica_groups=mesh['seq'=16,'chan'=2] {'seq'}, dimensions={0} | all-to-all | bytes 524288 | tf_op jit(solution)/shard_map/all_to_all | solution.py:224
  145.4 14.5 %shard_map.115 = (bf16[512,2048]{1,0:T(8,128)(2,1)}, bf16[512,2048]{1,0:T(8,128)(2,1)}) custom-call(bf16[512,2048]{1,0:T(8,128)(2,1)} %key_ref.5, bf16[512,2048]{1,0:T(8,128)(2,1)} %value_ref.5, f32[512,2048]{1,0:T(8,128)} %get-tuple-element.20.conv_ref, f32[16,2048]{1,0:T(8,128)} %get-tuple-element.27.rate_ref, f32[16,2048]{1,0:T(8,128)} %get-tuple-element.26.gain_ref, ...), custom_call_target="tpu_custom_call" | custom-call | flops 33554432 | bytes 14155776 | tf_op jit(solution)/shard_map/pallas_call | solution.py:306
  159.9 0.8 fusion
  (8 shorter events, 0.0 us)
Async XLA Ops:
  7.2 41.3 %all-gather.2.cloned.1.call-start = ((), (), s32[]{:S(2)}) async-start(), calls=%async_computation.5 | async-start | bytes 6291456 | tf_op jit(solution)/shard_map/all_gather | solution.py:355
  26.5 16.2 %all-to-all-start = ((f32[16,1,16,128]{3,2,1,0:T(8,128)}), f32[16,1,16,128]{3,2,1,0:T(8,128)S(1)}, u32[]{:S(2)}, u32[]{:S(2)}) async-start(f32[16,1,16,128]{3,2,1,0:T(8,128)} %get-tuple-element.17), calls=%async_computation | async-start | bytes 262144 | tf_op jit(solution)/shard_map/all_to_all | solution.py:224
  42.6 0.6 copy-start.1
  44.9 18.7 %all-to-all-start.1 = ((f32[16,1,16,128]{3,2,1,0:T(8,128)}), f32[16,1,16,128]{3,2,1,0:T(8,128)S(1)}, u32[]{:S(2)}, u32[]{:S(2)}) async-start(f32[16,1,16,128]{3,2,1,0:T(8,128)} %shard_map.111), calls=%async_computation.1 | async-start | bytes 262144 | tf_op jit(solution)/shard_map/all_to_all | solution.py:224
  48.4 112.3 %reduce-scatter.2.cloned.1.call-start = ((), (), s32[]{:S(2)}) async-start(), calls=%async_computation.6 | async-start | bytes 6291456 | tf_op jit(solution)/shard_map/reduce_scatter | solution.py:397
  63.6 0.7 copy-start.2
  145.4 14.5 %copy-start = (f32[16,2,16,128]{3,2,1,0:T(8,128)S(1)}, f32[16,2,16,128]{3,2,1,0:T(8,128)}, u32[]{:S(2)}) copy-start(f32[16,2,16,128]{3,2,1,0:T(8,128)} %all_to_all.21.carry_ref) | copy-start | bytes 786436
  145.4 14.5 %copy-start.3 = (f32[2048,16]{0,1:T(8,128)S(1)}, f32[2048,16]{0,1:T(8,128)}, u32[]{:S(2)}) copy-start(f32[2048,16]{0,1:T(8,128)} %param.10) | copy-start | bytes 393220
Sparse Core Ops, SparseCore 0:
  9.5 16.3 all-gather.1
  93.6 13.2 reduce-scatter.1

commit v3 on v2

--- a/solution.py
+++ b/solution.py
@@ -8,6 +8,7 @@
 from jax.sharding import PartitionSpec as P
 
 LANES = 128
+WIDE = 256
 BLOCKS = 8
 F32 = jnp.float32
 BF16 = jnp.bfloat16
@@ -122,6 +123,7 @@
     rate_ref,
     gain_ref,
     forward_ends_ref,
+    forward_total_ref,
     conv_ref,
     ends_ref,
     summary_ref,
@@ -183,45 +185,96 @@
         total = total + block_rows(sums_ref, b, modes)
         total = total + decay * block_rows(forward_ends_ref, b, modes) * run
         run = run * step_decay + block_rows(ends_ref, b, modes)
-    summary_ref[0, 0] = run
-    summary_ref[0, 1] = total
-
-
-def forward_join_kernel(row_count, held, rate_ref, answer):
-    rate = rate_ref[...]
+    summary_ref[0, 0] = forward_total_ref[0, 0]
+    summary_ref[0, 1] = run
+    summary_ref[0, 2] = total
+
+
+def exchange_kernel(count, row_count, parts_ref, rate_ref, out_ref, held, answer, *sems):
+    me = lax.axis_index("seq")
+    barrier = pltpu.get_barrier_semaphore()
+
+    def peer(k):
+        return lax.rem(me + k, count)
+
+    def source(k):
+        return lax.rem(me + count - k, count)
+
+    def greet(k, carry):
+        pl.semaphore_signal(
+            barrier, inc=1, device_id={"seq": peer(k)}, device_id_type=pl.DeviceIdType.MESH
+        )
+        return carry
+
+    lax.fori_loop(1, count, greet, 0)
+    pl.semaphore_wait(barrier, count - 1)
+
+    def copy(k, src, dst, place, send, recv):
+        return pltpu.make_async_remote_copy(
+            src_ref=src.at[peer(k)],
+            dst_ref=dst.at[place],
+            send_sem=send.at[k],
+            recv_sem=recv.at[k],
+            device_id={"seq": peer(k)},
+            device_id_type=pl.DeviceIdType.MESH,
+        )
+
+    def start_all(src, dst, send, recv):
+        def one(k, carry):
+            copy(k, src, dst, me, send, recv).start()
+            return carry
+
+        lax.fori_loop(1, count, one, 0)
+
+    def wait_all(src, dst, send, recv):
+        def one(k, carry):
+            copy(k, src, dst, source(k), send, recv).wait_recv()
+            return carry
+
+        lax.fori_loop(1, count, one, 0)
+
+    def drain_all(src, dst, send, recv):
+        def one(k, carry):
+            copy(k, src, dst, me, send, recv).wait_send()
+            return carry
+
+        lax.fori_loop(1, count, one, 0)
+
+    start_all(parts_ref, held, sems[0], sems[1])
+    held[me] = parts_ref[me]
+    rate = rate_ref[me]
+    decay = jnp.exp(-rate)
     device_decay = jnp.exp(-rate * float(row_count))
+    wait_all(parts_ref, held, sems[0], sems[1])
     run = jnp.zeros_like(rate)
-    for e in range(held.shape[0]):
+    for e in range(count):
         answer[e, 0] = run
         run = run * device_decay + held[e, 0]
-
-
-def backward_join_kernel(row_count, held, forward_held, rate_ref, answer):
-    rate = rate_ref[...]
-    count = held.shape[0]
-    decay = jnp.exp(-rate)
-    device_decay = jnp.exp(-rate * float(row_count))
     run = jnp.zeros_like(rate)
     total = jnp.zeros_like(rate)
     for e in reversed(range(count)):
-        answer[e, 0] = run
-        total = total + held[e, 1] + decay * forward_held[e, 0] * run
-        run = run * device_decay + held[e, 0]
+        answer[e, 1] = run
+        total = total + held[e, 2] + decay * held[e, 0] * run
+        run = run * device_decay + held[e, 1]
     for e in range(count):
-        answer[e, 1] = total
-
-
-def join(kernel, row_count, arrays, out):
+        answer[e, 2] = total
+    start_all(answer, out_ref, sems[2], sems[3])
+    out_ref[me] = answer[me]
+    wait_all(answer, out_ref, sems[2], sems[3])
+    drain_all(parts_ref, held, sems[0], sems[1])
+    drain_all(answer, out_ref, sems[2], sems[3])
+
+
+def exchange(parts, rates, row_count):
+    count, kinds, modes, lanes = parts.shape
     return pl.pallas_call(
-        functools.partial(kernel, row_count),
-        out_shape=jax.ShapeDtypeStruct(out.shape, F32),
-        in_specs=[pl.BlockSpec(memory_space=pltpu.VMEM)] * len(arrays),
+        functools.partial(exchange_kernel, count, row_count),
+        out_shape=jax.ShapeDtypeStruct(parts.shape, F32),
+        in_specs=[pl.BlockSpec(memory_space=pltpu.VMEM)] * 2,
         out_specs=pl.BlockSpec(memory_space=pltpu.VMEM),
-    )(*arrays)
-
-
-def trade(chunks):
-    return lax.all_to_all(chunks, "seq", split_axis=0, concat_axis=0, tiled=True)
+        scratch_shapes=[pltpu.VMEM(parts.shape, F32)] * 2 + [pltpu.SemaphoreType.DMA((count,))] * 4,
+        compiler_params=pltpu.CompilerParams(collective_id=0, has_side_effects=True),
+    )(parts, rates)
 
 
 def forward_kernel(
@@ -277,7 +330,7 @@
     rate = rate_ref[...]
     modes = rate.shape[0]
     decay = jnp.exp(-rate)
-    fill_carries(carry_ref[0, 0], ends_ref, rate, steps, carries, True)
+    fill_carries(carry_ref[0, 1], ends_ref, rate, steps, carries, True)
     decays = spread_rows(decay, 0, modes)
     firsts = spread_rows(decay * gain_ref[...], 0, modes)
 
@@ -297,15 +350,27 @@
 
 
 def by_lanes(rows):
-    return pl.BlockSpec((rows, LANES), lambda i: (0, i))
+    return pl.BlockSpec((rows, WIDE), lambda i: (0, i))
+
+
+def each_group(kernel, scratch_count, *refs):
+    arrays, scratches = refs[: len(refs) - scratch_count], refs[len(refs) - scratch_count :]
+
+    def one(r, i):
+        if len(r.shape) == 2:
+            return r.at[:, i * LANES : (i + 1) * LANES]
+        return r.at[i] if len(r.shape) == 3 else r.at[i : i + 1]
+
+    for i in range(WIDE // LANES):
+        part = [one(r, i) for r in arrays]
+        kernel(*part, *scratches)
 
 
 def call(kernel, arrays, specs, outs, out_specs, scratch_rows, flops):
-    groups = arrays[0].shape[1] // LANES
     moved = sum(a.size * a.dtype.itemsize for a in list(arrays) + list(outs))
     return pl.pallas_call(
-        kernel,
-        grid=(groups,),
+        functools.partial(each_group, kernel, len(scratch_rows)),
+        grid=(arrays[0].shape[1] // WIDE,),
         in_specs=specs,
         out_specs=out_specs,
         out_shape=outs,
@@ -339,19 +404,17 @@
     modes = rate.shape[0]
     groups = width // LANES
     work = rows * width * modes
-    ends_shape = jax.ShapeDtypeStruct((modes * BLOCKS, width), F32)
+    wide_groups = WIDE // LANES
+    ends_shape = jax.ShapeDtypeStruct((groups, modes * BLOCKS, LANES), F32)
     total_shape = jax.ShapeDtypeStruct((groups, 1, modes, LANES), F32)
-    summary_shape = jax.ShapeDtypeStruct((groups, 2, modes, LANES), F32)
+    summary_shape = jax.ShapeDtypeStruct((groups, 3, modes, LANES), F32)
     narrow = jax.ShapeDtypeStruct((rows, width), BF16)
     wide = jax.ShapeDtypeStruct((rows, width), F32)
-    big, mode_spec, ends_spec = by_lanes(rows), by_lanes(modes), by_lanes(modes * BLOCKS)
-    total_spec = pl.BlockSpec((1, 1, modes, LANES), lambda i: (i, 0, 0, 0))
-    summary_spec = pl.BlockSpec((1, 2, modes, LANES), lambda i: (i, 0, 0, 0))
+    big, mode_spec = by_lanes(rows), by_lanes(modes)
+    ends_spec = pl.BlockSpec((wide_groups, modes * BLOCKS, LANES), lambda i: (i, 0, 0))
+    total_spec = pl.BlockSpec((wide_groups, 1, modes, LANES), lambda i: (i, 0, 0, 0))
+    summary_spec = pl.BlockSpec((wide_groups, 3, modes, LANES), lambda i: (i, 0, 0, 0))
     rate_groups = rate.reshape(modes, groups, LANES).transpose(1, 0, 2)[:, None]
-    own_rate = lax.dynamic_index_in_dim(
-        to_chunks(rate_groups, seq_count)[:, 0], lax.axis_index("seq"), 0, keepdims=False
-    )
-
     all_cotangent = lax.all_gather(cotangent, "chan", axis=1, tiled=True)
     forward_local, forward_ends, forward_total = call(
         forward_local_kernel,
@@ -362,32 +425,26 @@
         [rows],
         4 * work,
     )
-    forward_held = trade(to_chunks(forward_total, seq_count))
-    forward_answer = join(
-        forward_join_kernel, rows, (forward_held, own_rate), forward_held
-    )
-    forward_carry = from_chunks(trade(forward_answer), groups)
     grad_gated = lax.dot_general(
         all_cotangent, out_weight, (((1,), (1,)), ((), ())), preferred_element_type=F32
     )
     backward_local, backward_ends, summary = call(
         backward_local_kernel,
-        (key_in, value_in, query_in, grad_gated, rate, gain, forward_ends),
-        [big, big, big, big, mode_spec, mode_spec, ends_spec],
+        (key_in, value_in, query_in, grad_gated, rate, gain, forward_ends, forward_total),
+        [big, big, big, big, mode_spec, mode_spec, ends_spec, total_spec],
         [wide, ends_shape, summary_shape],
         [big, ends_spec, summary_spec],
         [rows] * 5 + [modes * BLOCKS],
         6 * work,
     )
-    backward_held = trade(to_chunks(summary, seq_count))
-    backward_answer = join(
-        backward_join_kernel, rows, (backward_held, forward_held, own_rate), backward_held
-    )
-    joined = from_chunks(trade(backward_answer), groups)
+    joined = from_chunks(
+        exchange(to_chunks(summary, seq_count), to_chunks(rate_groups, seq_count)[:, 0], rows),
+        groups,
+    )
     gated, query_grad = call(
         forward_kernel,
-        (query_in, grad_gated, forward_local, rate, gain, forward_ends, forward_carry),
-        [big, big, big, mode_spec, mode_spec, ends_spec, total_spec],
+        (query_in, grad_gated, forward_local, rate, gain, forward_ends, joined),
+        [big, big, big, mode_spec, mode_spec, ends_spec, summary_spec],
         [narrow, narrow],
         [big, big],
         [rows, modes * BLOCKS],
@@ -406,7 +463,7 @@
         [rows, modes * BLOCKS],
         2 * work,
     )
-    correlation = joined[:, 1].transpose(0, 2, 1).reshape(width, modes)
+    correlation = joined[:, 2].transpose(0, 2, 1).reshape(width, modes)
     residue_grad = norm_factor * correlation / jnp.sqrt(F32(rows * seq_count))
     return (mixed_out, query_grad, key_grad, value_grad, residue_grad)
 

time: 169 us -> 138 us (0.82)
  blocking collectives: 28.2 us -> 0 us
  Pallas kernels: 71.5 us -> 86.5 us
  starting transfers between devices: 12 us -> 0.08 us
  waiting for transfers between devices: 7.87 us -> 2.76 us
    all_to_all x2 -> x0, blocking collectives: 28.2 us -> none  [trade(): lax.all_to_all(chunks, 'seq', split_axis=0, concat_axis=0, tiled=True)]
    pallas_call x6 -> x5, Pallas kernels: 71.5 us -> 86.5 us  [the longest x4 60.1 us: call(): pl.pallas_call(functools.partial(each_group, kernel, len(scratch_rows)),...]
    all_to_all x2 -> x0, starting transfers between devices: 11.9 us -> none  [trade(): lax.all_to_all(chunks, 'seq', split_axis=0, concat_axis=0, tiled=True)]
    all_to_all x2 -> x0, waiting for transfers between devices: 7.15 us -> none  [trade(): lax.all_to_all(chunks, 'seq', split_axis=0, concat_axis=0, tiled=True)]
  transfers between devices with their start and end apart: 4 -> 2, of which waited for: 1 -> 2; matrix products, arithmetic and copies ran while one was open for 11% -> 3% of each run, Pallas kernels for 34% -> 19%
where the time goes in v3:
time: 138 us; the launch traced here: 137 us
  Pallas kernels  86.5 us (63%)
  matrix products  29.3 us (21%)
  between operations  14.1 us (10%)
  other arithmetic  3.51 us (3%)
  waiting for transfers between devices  2.76 us (2%)
    pallas_call x4, Pallas kernels, call(): pl.pallas_call(functools.partial(each_group, kernel, len(scratch_rows)),...  60.1 us
    pallas_call x1, Pallas kernels, exchange(): pl.pallas_call(functools.partial(exchange_kernel, count, row_count), out_...  26.4 us
    dot_general x1, matrix products, per_device(): lax.dot_general(all_cotangent, out_weight, (((1,), (1,)), ((), ())), pref...  15 us
    dot_general x1, matrix products, per_device(): partial_out = jnp.dot(gated, out_weight, preferred_element_type=F32)  14.3 us
  transfers between devices with their start and end apart: 2, of which 2 were waited for; matrix products, arithmetic and copies ran while one was open for 3% of the time, Pallas kernels for 19%

profile of v3, /device:TPU:0, one launch (start us, length us, event | category | flops | bytes accessed | tf_op | source)
XLA Modules:
  0.0 136.8 jit_solution(5929290417458929515)
XLA Ops:
  7.2 0.0 all-gather.2.cloned.1.call-start
  7.2 0.7 all-gather.2.cloned.1.call-update
  7.9 0.0 reduce-scatter.2.cloned.1.call-start
  7.9 1.7 %fusion.1 = (f32[2,16,8,128]{3,2,1,0:T(8,128)S(1)}, f32[16,2048]{1,0:T(8,128)}, f32[16,2048]{1,0:T(8,128)}) fusion(f32[2048,16]{0,1:T(8,128)} %param.10, f32[2048,16]{0,1:T(8,128)} %param.11), kind=kLoop, calls=%fused_computation.8 | loop fusion | flops 131072 | bytes 655360
  9.7 0.7 copy.18
  10.4 15.0 %shard_map.110 = (f32[512,2048]{1,0:T(8,128)}, f32[16,128,128]{2,1,0:T(8,128)}, f32[16,1,16,128]{3,2,1,0:T(8,128)}) custom-call(bf16[512,2048]{1,0:T(8,128)(2,1)} %refs_0_.7, bf16[512,2048]{1,0:T(8,128)(2,1)} %refs_1_.5, f32[16,2048]{1,0:T(8,128)} %get-tuple-element.27.refs_2_.refs_4_.refs_3_, f32[16,2048]{1,0:T(8,128)} %get-tuple-element.26.refs_3_.refs_5_.refs_4_), custom_call_target="tpu_custom_call" | custom-call | flops 67108864 | bytes 9830400 | tf_op jit(solution)/shard_map/pallas_call | solution.py:371
  25.4 0.5 all-gather.2.cloned.1.call-done
  25.9 15.0 %fusion.3.refs_3_.refs_1_ = f32[512,2048]{1,0:T(8,128)} fusion(bf16[512,4096]{1,0:T(8,128)(2,1)} %all-gather.2.cloned.1.call-done, bf16[2048,4096]{1,0:T(8,128)(2,1)} %param.12), kind=kOutput, calls=%fused_computation.10 | convolution fusion | flops 8589934592 | bytes 25165824 | tf_op jit(solution)/shard_map/dot_general | solution.py:428
  40.9 21.9 %shard_map.111 = (f32[512,2048]{1,0:T(8,128)}, f32[16,128,128]{2,1,0:T(8,128)}, f32[16,3,16,128]{3,2,1,0:T(8,128)}) custom-call(bf16[512,2048]{1,0:T(8,128)(2,1)} %refs_0_.7, bf16[512,2048]{1,0:T(8,128)(2,1)} %refs_1_.5, bf16[512,2048]{1,0:T(8,128)(2,1)} %refs_0_.6, f32[512,2048]{1,0:T(8,128)} %fusion.3.refs_3_.refs_1_, ...), custom_call_target="tpu_custom_call" | custom-call | flops 100663296 | bytes 17563648 | tf_op jit(solution)/shard_map/pallas_call | solution.py:371
  62.8 26.4 %shard_map.112.refs_6_ = f32[16,3,16,128]{3,2,1,0:T(8,128)} custom-call(f32[16,3,16,128]{3,2,1,0:T(8,128)} %get-tuple-element.18.parts_ref, f32[16,16,128]{2,1,0:T(8,128)} %bitcast.26), custom_call_target="tpu_custom_call" | custom-call | tf_op jit(solution)/shard_map/pallas_call | solution.py:270
  89.2 11.6 %shard_map.113 = (bf16[512,2048]{1,0:T(8,128)(2,1)}, bf16[512,2048]{1,0:T(8,128)(2,1)}) custom-call(bf16[512,2048]{1,0:T(8,128)(2,1)} %refs_0_.6, f32[512,2048]{1,0:T(8,128)} %fusion.3.refs_3_.refs_1_, f32[512,2048]{1,0:T(8,128)} %get-tuple-element.15.refs_2_, f32[16,2048]{1,0:T(8,128)} %get-tuple-element.27.refs_2_.refs_4_.refs_3_, ...), custom_call_target="tpu_custom_call" | custom-call | flops 33554432 | bytes 16384000 | tf_op jit(solution)/shard_map/pallas_call | solution.py:371
  100.8 14.3 %convolution_convert_fusion = bf16[512,4096]{1,0:T(8,128)(2,1)} fusion(bf16[512,2048]{1,0:T(8,128)(2,1)} %get-tuple-element.19, bf16[2048,4096]{1,0:T(8,128)(2,1)} %param.12), kind=kOutput, calls=%fused_computation | convolution fusion | flops 8592031744 | bytes 23068672 | tf_op jit(solution)/shard_map/dot_general | solution.py:453
  115.1 0.0 reduce-scatter.2.cloned.1.call-update
  115.1 0.0 copy-start
  115.1 11.6 %shard_map.114 = (bf16[512,2048]{1,0:T(8,128)(2,1)}, bf16[512,2048]{1,0:T(8,128)(2,1)}) custom-call(bf16[512,2048]{1,0:T(8,128)(2,1)} %refs_0_.7, bf16[512,2048]{1,0:T(8,128)(2,1)} %refs_1_.5, f32[512,2048]{1,0:T(8,128)} %get-tuple-element.21.refs_2_, f32[16,2048]{1,0:T(8,128)} %get-tuple-element.27.refs_2_.refs_4_.refs_3_, ...), custom_call_target="tpu_custom_call" | custom-call | flops 33554432 | bytes 14286848 | tf_op jit(solution)/shard_map/pallas_call | solution.py:371
  126.7 0.0 copy-done
  126.7 1.8 %fusion = f32[2048,16]{0,1:T(8,128)} fusion(f32[2048,16]{0,1:T(8,128)S(1)} %copy-done, f32[16,3,16,128]{3,2,1,0:T(8,128)} %shard_map.112.refs_6_), kind=kLoop, calls=%fused_computation.2 | loop fusion | flops 163840 | bytes 393216 | tf_op jit(solution)/shard_map/div | solution.py:467
  128.5 1.5 %reduce-scatter.2.cloned.1.call-done = bf16[512,2048]{1,0:T(8,128)(2,1)} async-done(((bf16[512,4096]{1,0:T(8,128)(2,1)}), bf16[512,2048]{1,0:T(8,128)(2,1)}) %reduce-scatter.2.cloned.1.call-update) | async-done | bytes 2097168 | tf_op jit(solution)/shard_map/reduce_scatter | solution.py:454
Async XLA Ops:
  7.2 18.8 %all-gather.2.cloned.1.call-start = ((), (), s32[]{:S(2)}) async-start(), calls=%async_computation.1 | async-start | bytes 6291456 | tf_op jit(solution)/shard_map/all_gather | solution.py:418
  7.9 122.1 %reduce-scatter.2.cloned.1.call-start = ((), (), s32[]{:S(2)}) async-start(), calls=%async_computation.2 | async-start | bytes 6291456 | tf_op jit(solution)/shard_map/reduce_scatter | solution.py:454
  115.1 11.6 %copy-start = (f32[2048,16]{0,1:T(8,128)S(1)}, f32[2048,16]{0,1:T(8,128)}, u32[]{:S(2)}) copy-start(f32[2048,16]{0,1:T(8,128)} %param.10) | copy-start | bytes 393220
Sparse Core Ops, SparseCore 0:
  9.5 16.3 all-gather.1
  115.2 14.7 reduce-scatter.1

commit v4 on v3

--- a/solution.py
+++ b/solution.py
@@ -8,7 +8,7 @@
 from jax.sharding import PartitionSpec as P
 
 LANES = 128
-WIDE = 256
+WIDE = 512
 BLOCKS = 8
 F32 = jnp.float32
 BF16 = jnp.bfloat16

time: 138 us -> 138 us (level)
  no operation moved by 1% of the time
where the time goes in v4:
time: 138 us; the launch traced here: 137 us
  Pallas kernels  86.1 us (62%)
  matrix products  29.3 us (21%)
  between operations  14.1 us (10%)
  waiting for transfers between devices  3.71 us (3%)
  other arithmetic  3.43 us (2%)
    pallas_call x4, Pallas kernels, call(): pl.pallas_call(functools.partial(each_group, kernel, len(scratch_rows)),...  59.3 us
    pallas_call x1, Pallas kernels, exchange(): pl.pallas_call(functools.partial(exchange_kernel, count, row_count), out_...  26.8 us
    dot_general x1, matrix products, per_device(): lax.dot_general(all_cotangent, out_weight, (((1,), (1,)), ((), ())), pref...  15 us
    dot_general x1, matrix products, per_device(): partial_out = jnp.dot(gated, out_weight, preferred_element_type=F32)  14.3 us
    reduce_scatter x1, waiting for transfers between devices, per_device(): lax.psum_scatter(partial_out.astype(BF16), 'chan', scatter_dimension=1, t...  2.84 us
  transfers between devices with their start and end apart: 2, of which 2 were waited for; matrix products, arithmetic and copies ran while one was open for 3% of the time, Pallas kernels for 19%

profile of v4, /device:TPU:0, one launch (start us, length us, event | category | flops | bytes accessed | tf_op | source)
XLA Modules:
  0.0 137.3 jit_solution(17972677710661666396)
XLA Ops:
  7.2 0.0 all-gather.2.cloned.1.call-start
  7.2 0.7 all-gather.2.cloned.1.call-update
  7.9 0.0 reduce-scatter.2.cloned.1.call-start
  7.9 1.7 %fusion.1 = (f32[2,16,8,128]{3,2,1,0:T(8,128)S(1)}, f32[16,2048]{1,0:T(8,128)}, f32[16,2048]{1,0:T(8,128)}) fusion(f32[2048,16]{0,1:T(8,128)} %param.10, f32[2048,16]{0,1:T(8,128)} %param.11), kind=kLoop, calls=%fused_computation.8 | loop fusion | flops 131072 | bytes 655360
  9.7 0.7 copy.18
  10.4 15.4 %shard_map.110 = (f32[512,2048]{1,0:T(8,128)}, f32[16,128,128]{2,1,0:T(8,128)}, f32[16,1,16,128]{3,2,1,0:T(8,128)}) custom-call(bf16[512,2048]{1,0:T(8,128)(2,1)} %refs_0_.7, bf16[512,2048]{1,0:T(8,128)(2,1)} %refs_1_.5, f32[16,2048]{1,0:T(8,128)} %get-tuple-element.27.refs_2_.refs_4_.refs_3_, f32[16,2048]{1,0:T(8,128)} %get-tuple-element.26.refs_3_.refs_5_.refs_4_), custom_call_target="tpu_custom_call" | custom-call | flops 67108864 | bytes 9830400 | tf_op jit(solution)/shard_map/pallas_call | solution.py:371
  25.8 0.2 all-gather.2.cloned.1.call-done
  25.9 15.0 %fusion.3.refs_3_.refs_1_ = f32[512,2048]{1,0:T(8,128)} fusion(bf16[512,4096]{1,0:T(8,128)(2,1)} %all-gather.2.cloned.1.call-done, bf16[2048,4096]{1,0:T(8,128)(2,1)} %param.12), kind=kOutput, calls=%fused_computation.10 | convolution fusion | flops 8589934592 | bytes 25165824 | tf_op jit(solution)/shard_map/dot_general | solution.py:428
  40.9 22.8 %shard_map.111 = (f32[512,2048]{1,0:T(8,128)}, f32[16,128,128]{2,1,0:T(8,128)}, f32[16,3,16,128]{3,2,1,0:T(8,128)}) custom-call(bf16[512,2048]{1,0:T(8,128)(2,1)} %refs_0_.7, bf16[512,2048]{1,0:T(8,128)(2,1)} %refs_1_.5, bf16[512,2048]{1,0:T(8,128)(2,1)} %refs_0_.6, f32[512,2048]{1,0:T(8,128)} %fusion.3.refs_3_.refs_1_, ...), custom_call_target="tpu_custom_call" | custom-call | flops 100663296 | bytes 17563648 | tf_op jit(solution)/shard_map/pallas_call | solution.py:371
  63.7 26.8 %shard_map.112.refs_6_ = f32[16,3,16,128]{3,2,1,0:T(8,128)} custom-call(f32[16,3,16,128]{3,2,1,0:T(8,128)} %get-tuple-element.18.parts_ref, f32[16,16,128]{2,1,0:T(8,128)} %bitcast.26), custom_call_target="tpu_custom_call" | custom-call | tf_op jit(solution)/shard_map/pallas_call | solution.py:270
  90.5 10.8 %shard_map.113 = (bf16[512,2048]{1,0:T(8,128)(2,1)}, bf16[512,2048]{1,0:T(8,128)(2,1)}) custom-call(bf16[512,2048]{1,0:T(8,128)(2,1)} %refs_0_.6, f32[512,2048]{1,0:T(8,128)} %fusion.3.refs_3_.refs_1_, f32[512,2048]{1,0:T(8,128)} %get-tuple-element.15.refs_2_, f32[16,2048]{1,0:T(8,128)} %get-tuple-element.27.refs_2_.refs_4_.refs_3_, ...), custom_call_target="tpu_custom_call" | custom-call | flops 33554432 | bytes 16384000 | tf_op jit(solution)/shard_map/pallas_call | solution.py:371
  101.2 14.3 %convolution_convert_fusion = bf16[512,4096]{1,0:T(8,128)(2,1)} fusion(bf16[512,2048]{1,0:T(8,128)(2,1)} %get-tuple-element.19, bf16[2048,4096]{1,0:T(8,128)(2,1)} %param.12), kind=kOutput, calls=%fused_computation | convolution fusion | flops 8592031744 | bytes 23068672 | tf_op jit(solution)/shard_map/dot_general | solution.py:453
  115.6 0.0 reduce-scatter.2.cloned.1.call-update
  115.6 0.0 copy-start
  115.6 10.3 %shard_map.114 = (bf16[512,2048]{1,0:T(8,128)(2,1)}, bf16[512,2048]{1,0:T(8,128)(2,1)}) custom-call(bf16[512,2048]{1,0:T(8,128)(2,1)} %refs_0_.7, bf16[512,2048]{1,0:T(8,128)(2,1)} %refs_1_.5, f32[512,2048]{1,0:T(8,128)} %get-tuple-element.21.refs_2_, f32[16,2048]{1,0:T(8,128)} %get-tuple-element.27.refs_2_.refs_4_.refs_3_, ...), custom_call_target="tpu_custom_call" | custom-call | flops 33554432 | bytes 14286848 | tf_op jit(solution)/shard_map/pallas_call | solution.py:371
  126.0 0.0 copy-done
  126.0 1.7 %fusion = f32[2048,16]{0,1:T(8,128)} fusion(f32[2048,16]{0,1:T(8,128)S(1)} %copy-done, f32[16,3,16,128]{3,2,1,0:T(8,128)} %shard_map.112.refs_6_), kind=kLoop, calls=%fused_computation.2 | loop fusion | flops 163840 | bytes 393216 | tf_op jit(solution)/shard_map/div | solution.py:467
  127.7 2.8 %reduce-scatter.2.cloned.1.call-done = bf16[512,2048]{1,0:T(8,128)(2,1)} async-done(((bf16[512,4096]{1,0:T(8,128)(2,1)}), bf16[512,2048]{1,0:T(8,128)(2,1)}) %reduce-scatter.2.cloned.1.call-update) | async-done | bytes 2097168 | tf_op jit(solution)/shard_map/reduce_scatter | solution.py:454
Async XLA Ops:
  7.2 18.8 %all-gather.2.cloned.1.call-start = ((), (), s32[]{:S(2)}) async-start(), calls=%async_computation.1 | async-start | bytes 6291456 | tf_op jit(solution)/shard_map/all_gather | solution.py:418
  7.9 122.6 %reduce-scatter.2.cloned.1.call-start = ((), (), s32[]{:S(2)}) async-start(), calls=%async_computation.2 | async-start | bytes 6291456 | tf_op jit(solution)/shard_map/reduce_scatter | solution.py:454
  115.6 10.4 %copy-start = (f32[2048,16]{0,1:T(8,128)S(1)}, f32[2048,16]{0,1:T(8,128)}, u32[]{:S(2)}) copy-start(f32[2048,16]{0,1:T(8,128)} %param.10) | copy-start | bytes 393220
Sparse Core Ops, SparseCore 0:
  9.5 16.3 all-gather.1
  115.7 14.7 reduce-scatter.1
